TPU v7x, 128 devices: a whole 4x4x4 slice. The times are simulated.
128 devices in a mesh: leaf: 128 (over x, z, y, core).
Axes of the slice: x: 4, y: 4, z: 4, core: 2. Of those that a mesh axis runs over, the one named last changes fastest.
Arguments:
- density: bfloat16 [256, 24, 28, 512], P('leaf'), may hold values from 0.25 to 450
- occupied: int32 [128, 12, 14], P('leaf'), may hold values 0 or 1
- anterpolate: bfloat16 [512, 128], replicated, may hold values from -0.25 to 0.25
- merge_tables: bfloat16 [8, 128, 128], replicated, may hold values from -0.5 to 0.5
- transfer_tables: bfloat16 [158, 128, 128], replicated, may hold values from -0.0390625 to 0.0390625
- near_tables: bfloat16 [14, 512, 512], replicated, may hold values from -0.0546875 to 0.0546875
Outputs:
- potential: bfloat16 [256, 24, 28, 512], P('leaf')
All inputs are finite; a program needn't handle non-finite values. No bound on the sum of `occupied` on one device may be relied on, other than what follows from the above.
Results may differ from a plain program's by a relative error of at most 0.014.
Values may be sent and summed in bfloat16 or wider, within the bound.
No kernel may reach another device: no remote copies, remote signals or barrier semaphores. Data moves between devices by JAX's collectives and lax.ppermute only.
A program may use at most 192 MiB of HBM per device.

v0:
```python
import jax
import jax.numpy as jnp
import numpy as np
from jax import lax
from jax.experimental import pallas as pl
from jax.experimental.pallas import tpu as pltpu
from jax.sharding import PartitionSpec as P

F32 = jnp.float32
BF16 = jnp.bfloat16
GROUP = 16
LINES = 12
ROWS = GROUP * LINES
PTS = 512
K = 128
COARSE = 48
VMEM = pl.BlockSpec(memory_space=pltpu.VMEM)
SMEM = pl.BlockSpec(memory_space=pltpu.SMEM)


def mul(a, b):
    return jnp.dot(a, b, preferred_element_type=F32)


def mul_t(a, b):
    return lax.dot_general(a, b, (((1,), (1,)), ((), ())), preferred_element_type=F32)


def wide(column):
    return jnp.concatenate([column] * 4, axis=1)


def prologue_kernel(density, mask, anterpolate, merge, low, high, parents, partial, stage):
    stage[...] = jnp.zeros_like(stage)
    packs = (low, high)

    def line(yp, total):
        rows = pl.ds(pl.multiple_of(yp * GROUP, GROUP), GROUP)
        present = wide(mask[rows, :])
        for z in range(2):
            for py in range(2):
                for h in range(4):
                    stage[z * 8 + py * 4 + h, 0:28, :] = density[z, 2 * yp + py, :, h * 128 : h * 128 + 128].astype(F32)
        for z in range(2):
            for py in range(2):
                for px in range(2):
                    part = jnp.concatenate(
                        [stage[z * 8 + py * 4 + h, pl.ds(px, GROUP, stride=2), :] for h in range(4)], axis=1
                    )
                    part = part * present
                    total = total + part
                    packs[z][py * 2 + px, rows, 0:PTS] = part.astype(BF16)
        return total

    total = lax.fori_loop(0, LINES, line, jnp.zeros((GROUP, PTS), F32))
    partial[...] = jnp.broadcast_to(jnp.sum(total), partial.shape)
    for z in range(2):
        found = mul(packs[z][:, :, 0:PTS].reshape(4 * ROWS, PTS), anterpolate[...]).astype(BF16)
        found = found.reshape(4, ROWS, K)
        low[:, :, PTS + z * K : PTS + z * K + K] = found
        high[:, :, PTS + z * K : PTS + z * K + K] = found
    parents[...] = merged(low, merge)


def merged(pack, merge):
    children = [pack[c % 4, :, PTS + (c // 4) * K : PTS + (c // 4) * K + K] for c in range(8)]
    return mul(jnp.concatenate(children, axis=1), merge[...]).astype(BF16)


def prologue(density, mask, anterpolate, merge):
    pack = jax.ShapeDtypeStruct((4, ROWS, PTS + 2 * K), BF16)
    return pl.pallas_call(
        prologue_kernel,
        name="prologue",
        out_shape=(
            pack,
            pack,
            jax.ShapeDtypeStruct((ROWS, K), BF16),
            jax.ShapeDtypeStruct((128, 128), F32),
        ),
        in_specs=[VMEM] * 4,
        out_specs=(VMEM,) * 4,
        scratch_shapes=[pltpu.VMEM((16, 32, 128), F32)],
        compiler_params=pltpu.CompilerParams(vmem_limit_bytes=32 << 20),
    )(density, mask, anterpolate, merge)


KEPT = [(3, 0), (3, 1), (3, 2), (3, 3), (1, 3), (2, 3), (1, 1), (1, 2), (2, 1), (2, 2)]
MIRROR = (3, 1, 2, 0)


def taps(before, centre, after):
    ends = before + after
    return [before, 0.5 * (ends + centre), 0.5 * (ends - centre), after]


def outer_weights(tables, outer):
    def chunk(r, _):
        rows = pl.ds(pl.multiple_of(r * 16, 16), 16)
        for h in range(4):
            lanes = slice(h * 128, h * 128 + 128)
            g = [tables[5 + n, rows, lanes].astype(F32) for n in range(9)]
            along_x = [taps(*g[3 * y : 3 * y + 3]) for y in range(3)]
            for c in range(4):
                along_y = taps(along_x[0][c], along_x[1][c], along_x[2][c])
                for b in range(4):
                    outer[b * 4 + c, rows, lanes] = along_y[b].astype(BF16)
        return 0

    lax.fori_loop(0, PTS // 16, chunk, 0)


def inner_weights(tables, outer, inner):
    def block(n, _):
        here = pl.ds(pl.multiple_of((n // 4) * 128, 128), 128)
        there = pl.ds(pl.multiple_of((n % 4) * 128, 128), 128)
        t = [tables[m, here, there].astype(F32) for m in range(5)]
        f = [None] + [tables[m, there, here].astype(F32).T for m in range(1, 5)]
        above = taps(t[2], t[3], t[4])
        below = taps(f[4], f[3], f[2])
        level = taps(f[1], t[0], t[1])
        for k, (b, c) in enumerate(KEPT):
            if b == 3:
                flat = above[c]
            elif b == 1:
                flat = 0.5 * (below[c] + above[c] + level[c])
            else:
                flat = 0.5 * (below[c] + above[c] - level[c])
            ends = outer[b * 4 + c, here, there].astype(F32)
            ends = ends + outer[MIRROR[b] * 4 + MIRROR[c], there, here].astype(F32).T
            inner[k, here, there] = (0.5 * (ends + flat)).astype(BF16)
            inner[10 + k, here, there] = (0.5 * (ends - flat)).astype(BF16)
        return 0

    lax.fori_loop(0, 16, block, 0)


def spread_line(load, store):
    along_y = []
    for px in range(2):
        d0 = load(1, px, -1)
        d1 = load(0, px, 0)
        d2 = load(1, px, 0)
        d3 = load(0, px, 1)
        along_y.append((d0 - d2, d1 + d2, d2 - d1, d1 - d3))
    for b in range(4):
        even = along_y[0][b]
        odd = along_y[1][b]
        store(b * 4 + 0, pltpu.roll(odd, 1, axis=0) - odd)
        store(b * 4 + 1, even + odd)
        store(b * 4 + 2, odd - even)
        store(b * 4 + 3, even - pltpu.roll(even, GROUP - 1, axis=0))


def spread(first, second, combine, spread_ref, base):
    def line(yp, _):
        rows = pl.ds(pl.multiple_of(yp * GROUP, GROUP), GROUP)
        for h in range(4):
            lanes = slice(h * 128, h * 128 + 128)

            def load(py, px, shift):
                near_line = jnp.clip(yp + shift, 0, LINES - 1)
                at = pl.ds(pl.multiple_of(near_line * GROUP, GROUP), GROUP)
                found = combine(
                    first[py * 2 + px, at, lanes].astype(F32), second[py * 2 + px, at, lanes].astype(F32)
                )
                if shift == 0:
                    return found
                inside = (yp + shift >= 0) & (yp + shift < LINES)
                return jnp.where(inside, found, 0.0)

            def store(n, value):
                spread_ref[base + n, rows, lanes] = value.astype(BF16)

            spread_line(load, store)
        return 0

    lax.fori_loop(0, LINES, line, 0)


def gathered_products(product, held, made):
    for b in range(4):
        for c in range(4):
            made[c] = product(b, c)
        p = [made[c] for c in range(4)]
        sides = (p[0] + p[1] + p[2], p[1] - p[2] - p[3])
        for px in range(2):
            value = sides[px]
            if b == 0:
                held[0, px] = value
            elif b == 1:
                held[0, px] += value
                held[1, px] = value
            elif b == 2:
                held[0, px] += value
                held[1, px] -= value
            else:
                held[1, px] -= value


def near_inner_kernel(low, high, tables, near, outer, parts, inner, held, made):
    outer_weights(tables, outer)
    inner_weights(tables, outer, inner)
    spread(low, high, lambda d1, d2: d1 + d2, parts, 0)
    spread(low, high, lambda d1, d2: d2 - d1, parts, 16)

    def product(a):
        def one(b, c):
            left = parts[a * 16 + b * 4 + c]
            if (b, c) in KEPT:
                return mul(left, inner[a * 10 + KEPT.index((b, c))])
            return mul_t(left, inner[a * 10 + KEPT.index((MIRROR[b], MIRROR[c]))])

        return one

    gathered_products(product(0), held, made)
    near[0] = held[...]
    near[1] = held[...]
    gathered_products(product(1), held, made)
    near[0] += held[...]
    near[1] -= held[...]


def near_inner(low, high, tables):
    return pl.pallas_call(
        near_inner_kernel,
        name="near_inner",
        out_shape=(
            jax.ShapeDtypeStruct((2, 2, 2, ROWS, PTS), F32),
            jax.ShapeDtypeStruct((16, PTS, PTS), BF16),
        ),
        in_specs=[VMEM] * 3,
        out_specs=(VMEM,) * 2,
        scratch_shapes=[
            pltpu.VMEM((32, ROWS, PTS), BF16),
            pltpu.VMEM((20, PTS, PTS), BF16),
            pltpu.VMEM((2, 2, ROWS, PTS), F32),
            pltpu.VMEM((4, ROWS, PTS), F32),
        ],
        cost_estimate=pl.CostEstimate(flops=10_000_000_000, bytes_accessed=20_000_000, transcendentals=0),
        compiler_params=pltpu.CompilerParams(vmem_limit_bytes=60 << 20),
    )(low, high, tables)


def near_outer_kernel(kept, low, high, below, above, outer, near_in, near, parts, held, made):
    spread(below, high, lambda d0, d2: d0 * kept[0] - d2, parts, 0)
    spread(low, above, lambda d1, d3: d1 - d3 * kept[1], parts, 16)
    gathered_products(
        lambda b, c: mul_t(parts[b * 4 + c], outer[MIRROR[b] * 4 + MIRROR[c]]), held, made
    )
    near[0] = near_in[0] + held[...]
    gathered_products(lambda b, c: mul(parts[16 + b * 4 + c], outer[b * 4 + c]), held, made)
    near[1] = near_in[1] - held[...]


def near_outer(kept, low, high, below, above, outer, near):
    return pl.pallas_call(
        near_outer_kernel,
        name="near_outer",
        out_shape=jax.ShapeDtypeStruct((2, 2, 2, ROWS, PTS), F32),
        in_specs=[SMEM] + [VMEM] * 6,
        out_specs=VMEM,
        scratch_shapes=[
            pltpu.VMEM((32, ROWS, PTS), BF16),
            pltpu.VMEM((2, 2, ROWS, PTS), F32),
            pltpu.VMEM((4, ROWS, PTS), F32),
        ],
        cost_estimate=pl.CostEstimate(flops=7_000_000_000, bytes_accessed=20_000_000, transcendentals=0),
        compiler_params=pltpu.CompilerParams(vmem_limit_bytes=60 << 20),
    )(kept, low, high, below, above, outer, near)


def positive_offsets(radius, minimum):
    reach = range(-radius, radius + 1)
    return [
        (z, y, x)
        for z in reach
        for y in reach
        for x in reach
        if max(abs(z), abs(y), abs(x)) >= minimum and (z, y, x) > (0, 0, 0)
    ]


RANK = {offset: row for row, offset in enumerate(positive_offsets(3, 2))}


def transfer_terms(tables, dz, reach, py, source):
    plain, flipped = ([], []), ([], [])
    blank = jnp.zeros((K, K), BF16)
    for jy in reach:
        dy = jy - py
        for jx in range(-2, 4):
            pair = []
            for px in range(2):
                offset = (dz, dy, jx - px)
                other = tuple(-d for d in offset)
                pair.append((RANK.get(offset), RANK.get(other)))
            left = None
            for way, kept in ((0, plain), (1, flipped)):
                if pair[0][way] is None and pair[1][way] is None:
                    continue
                left = source(jy, jx) if left is None else left
                kept[0].append(left)
                kept[1].append(
                    jnp.concatenate(
                        [blank if q[way] is None else tables[q[way]] for q in pair], axis=1 - way
                    )
                )
    terms = []
    if plain[0]:
        terms.append(mul(jnp.concatenate(plain[0], axis=1), jnp.concatenate(plain[1], axis=0)))
    if flipped[0]:
        terms.append(mul_t(jnp.concatenate(flipped[0], axis=1), jnp.concatenate(flipped[1], axis=1)))
    return terms


def neighbours(even, odd, count):
    return jnp.concatenate(
        [
            pltpu.roll(even, 1, axis=0),
            pltpu.roll(odd, 1, axis=0),
            even,
            odd,
            pltpu.roll(even, count - 1, axis=0),
            pltpu.roll(odd, count - 1, axis=0),
        ],
        axis=1,
    ).astype(BF16)


def coarse_lines(box, stage, slot, lines):
    stage[...] = box
    sides = []
    for py in range(2):
        halves = []
        for px in range(2):
            halves.append(
                jnp.concatenate(
                    [stage[pl.ds(32 * g + 16 * py + px, 8, stride=2), :] for g in range(6)], axis=0
                )
            )
        sides.append(halves)
    blank = jnp.zeros((8, K), F32)
    for jy in range(-2, 4):
        even, odd = sides[jy % 2]
        if jy // 2 < 0:
            even, odd = [jnp.concatenate([blank, h[: COARSE - 8]], axis=0) for h in (even, odd)]
        elif jy // 2 > 0:
            even, odd = [jnp.concatenate([h[8:], blank], axis=0) for h in (even, odd)]
        lines[slot, jy + 2] = neighbours(even, odd, COARSE)


def transfer_kernel(
    parity, kept, low, below, above, own, back2, ahead2, far3, mask, charge, merge, anterpolate, tables, near,
    potential, leaves, lines, stage, weave, coarse,
):
    packs = (below, below, low, low, above, above)
    leaves[...] = jnp.zeros_like(leaves)
    for n in range(6):
        first = PTS + (n % 2) * K
        for py in range(2):
            even = packs[n][py * 2, :, first : first + K].astype(F32)
            odd = packs[n][py * 2 + 1, :, first : first + K].astype(F32)
            if n < 2 or n > 3:
                even, odd = even * kept[n // 4], odd * kept[n // 4]
            leaves[n, py, GROUP : GROUP + ROWS, :] = neighbours(even, odd, ROWS)
    side = parity[0]
    boxes = (back2[...], merged(below, merge), own[...], merged(above, merge), ahead2[...])
    for n, (box, flag) in enumerate(zip(boxes, (2, 0, None, 1, 3))):
        box = box.astype(F32)
        coarse_lines(box if flag is None else box * kept[flag], stage, n + side, lines)
    coarse_lines(far3[...].astype(F32) * kept[4], stage, 5 - 5 * side, lines)

    for pz in range(2):

        @pl.when(side == pz)
        def _():
            for py in range(2):
                total = None
                for jz in range(-2, 4):
                    for term in transfer_terms(
                        tables,
                        jz - pz,
                        range(-2, 4),
                        py,
                        lambda jy, jx: lines[jz + 2, jy + 2, :, (jx + 2) * K : (jx + 3) * K],
                    ):
                        total = term if total is None else total + term
                coarse[py] = 0.5 * total

    for py in range(2):
        for px in range(2):
            for g in range(6):
                stage[pl.ds(32 * g + 16 * py + px, 8, stride=2), :] = coarse[
                    py, g * 8 : g * 8 + 8, px * K : px * K + K
                ]
    parent_local = stage[...].astype(BF16)

    total_charge = jnp.sum(charge[...], axis=0, keepdims=True)
    leaf_count = 2.0 * 24 * 28 * 128
    factor = wide(mask[...] * (leaf_count * PTS / total_charge))

    for pz in range(2):
        for py in range(2):
            total = mul_t(parent_local, merge[(4 * pz + 2 * py) * K : (4 * pz + 2 * py) * K + 2 * K, :])
            for jz in range(-2, 4):
                for term in transfer_terms(
                    tables,
                    jz - pz,
                    range(-2, 4),
                    py,
                    lambda jy, jx: leaves[
                        jz + 2,
                        jy % 2,
                        GROUP * (1 + jy // 2) : GROUP * (1 + jy // 2) + ROWS,
                        (jx + 2) * K : (jx + 3) * K,
                    ],
                ):
                    total = total + term
            local = total.astype(BF16)
            for px in range(2):
                far = mul_t(local[:, px * K : px * K + K], anterpolate[...])
                found = (near[pz, py, px] + far) * factor
                for yp in range(LINES):
                    for h in range(4):
                        weave[yp * 4 + h, pl.ds(px, GROUP, stride=2), :] = found[
                            yp * GROUP : yp * GROUP + GROUP, h * 128 : h * 128 + 128
                        ]
            for yp in range(LINES):
                for h in range(4):
                    potential[pz, 2 * yp + py, :, h * 128 : h * 128 + 128] = weave[yp * 4 + h, 0:28, :].astype(BF16)


def transfer(parity, kept, low, below, above, own, back2, ahead2, far3, mask, charge, merge, anterpolate, tables, near):
    return pl.pallas_call(
        transfer_kernel,
        name="transfer",
        out_shape=jax.ShapeDtypeStruct((2, 2 * LINES, 28, PTS), BF16),
        in_specs=[SMEM] * 2 + [VMEM] * 13,
        out_specs=VMEM,
        scratch_shapes=[
            pltpu.VMEM((6, 2, ROWS + 2 * GROUP, 6 * K), BF16),
            pltpu.VMEM((6, 6, COARSE, 6 * K), BF16),
            pltpu.VMEM((ROWS, K), F32),
            pltpu.VMEM((LINES * 4, 32, 128), F32),
            pltpu.VMEM((2, COARSE, 2 * K), F32),
        ],
        cost_estimate=pl.CostEstimate(flops=12_000_000_000, bytes_accessed=20_000_000, transcendentals=0),
        compiler_params=pltpu.CompilerParams(vmem_limit_bytes=60 << 20),
    )(parity, kept, low, below, above, own, back2, ahead2, far3, mask, charge, merge, anterpolate, tables, near)


def around(count, step):
    return [(i, (i + step) % count) for i in range(count)]


def body(density, occupied, anterpolate, merge_tables, transfer_tables, near_tables):
    count = lax.axis_size("leaf")
    present = jnp.pad(occupied[0].astype(F32), ((0, 0), (0, GROUP - occupied.shape[2])))
    mask = jnp.broadcast_to(present.reshape(ROWS, 1), (ROWS, 128))
    merge = merge_tables.reshape(8 * K, K)
    low, high, own, partial = prologue(density, mask, anterpolate, merge)
    place = lax.axis_index("leaf")
    below = lax.ppermute(high, "leaf", around(count, 1))
    above = lax.ppermute(low, "leaf", around(count, -1))
    back2 = lax.ppermute(own, "leaf", around(count, 2))
    ahead2 = lax.ppermute(own, "leaf", around(count, -2))
    crossed = [(i, (i + 3) % count) for i in range(0, count, 2)]
    far3 = lax.ppermute(own, "leaf", crossed + [(j, i) for i, j in crossed])
    charge = lax.all_to_all(partial, "leaf", 0, 0, tiled=True)
    parity = place % 2
    source3 = place + 3 - 6 * parity
    kept = jnp.stack(
        [place >= 1, place < count - 1, place >= 2, place < count - 2, (source3 >= 0) & (source3 < count)]
    ).astype(F32)
    near, outer = near_inner(low, high, near_tables)
    near = near_outer(kept, low, high, below, above, outer, near)
    return transfer(
        parity.reshape(1), kept, low, below, above, own, back2, ahead2, far3, mask, charge, merge, anterpolate,
        transfer_tables, near,
    )


def solution(mesh):
    return jax.shard_map(
        body,
        mesh=mesh,
        in_specs=(P("leaf", None, None, None), P("leaf", None, None), P(), P(), P(), P()),
        out_specs=P("leaf", None, None, None),
        check_vma=False,
    )
```

profile of v0, /device:TPU:1, one launch (start us, length us, event | category | flops | bytes accessed | tf_op | source)
XLA Modules:
  0.0 109.0 jit_solution(4505094703419878167)
XLA Ops:
  0.0 0.7 convert_element_type.12
  0.8 0.1 broadcast_in_dim.7
  0.8 1.8 %copy.9.density = bf16[2,24,28,512]{3,2,1,0:T(8,128)(2,1)S(1)} copy(bf16[2,24,28,512]{3,1,2,0:T(8,128)(2,1)} %param.6) | data formatting | bytes 2752512 | tf_op args[0]
  2.7 0.1 broadcast_in_dim.8.mask
  2.8 1.8 %prologue.1 = (bf16[4,192,768]{2,1,0:T(8,128)(2,1)S(1)}, bf16[4,192,768]{2,1,0:T(8,128)(2,1)S(1)}, bf16[192,128]{1,0:T(8,128)(2,1)S(1)}, f32[128,128]{1,0:T(8,128)}) custom-call(bf16[2,24,28,512]{3,2,1,0:T(8,128)(2,1)S(1)} %copy.9.density, f32[192,128]{1,0:T(8,128)S(1)} %broadcast_in_dim.8.mask, bf16[512,128]{1,0:T(8,128)(2,1)S(1)} %copy-done.2, ...), custom_call_target="tpu_custom_call" | custom-call | tf_op jit(solution)/shard_map/prologue/pallas_call | solution.py:72
  4.6 1.4 %collective-permute-start.1 = (bf16[4,192,768]{2,1,0:T(8,128)(2,1)S(1)}, bf16[4,192,768]{2,1,0:T(8,128)(2,1)}, u32[]{:S(2)}, u32[]{:S(2)}) collective-permute-start(bf16[4,192,768]{2,1,0:T(8,128)(2,1)S(1)} %get-tuple-element.11.low), channel_id=1, source_target_pairs={{0,127},{1,0},{2,1},{3,2},{4,3},{5,4},{6,5},{7,6},{8,7},{9,8},{10,... | collective-permute-start | bytes 3538952 | tf_op jit(solution)/shard_map/ppermute | solution.py:465
  6.0 1.3 %collective-permute-start = (bf16[4,192,768]{2,1,0:T(8,128)(2,1)S(1)}, bf16[4,192,768]{2,1,0:T(8,128)(2,1)}, u32[]{:S(2)}, u32[]{:S(2)}) collective-permute-start(bf16[4,192,768]{2,1,0:T(8,128)(2,1)S(1)} %get-tuple-element.12.high), channel_id=1, source_target_pairs={{0,1},{1,2},{2,3},{3,4},{4,5},{5,6},{6,7},{7,8},{8,9},{9,10},{10,1... | collective-permute-start | bytes 3538952 | tf_op jit(solution)/shard_map/ppermute | solution.py:464
  7.4 1.3 %collective-permute-start.2 = (bf16[192,128]{1,0:T(8,128)(2,1)S(1)}, bf16[192,128]{1,0:T(8,128)(2,1)S(1)}, u32[]{:S(2)}, u32[]{:S(2)}) collective-permute-start(bf16[192,128]{1,0:T(8,128)(2,1)S(1)} %get-tuple-element.13.own), channel_id=1, source_target_pairs={{0,2},{1,3},{2,4},{3,5},{4,6},{5,7},{6,8},{7,9},{8,10},{9,11},{10,... | collective-permute-start | bytes 147464 | tf_op jit(solution)/shard_map/ppermute | solution.py:466
  8.7 12.3 %collective-permute-start.3 = (bf16[192,128]{1,0:T(8,128)(2,1)S(1)}, bf16[192,128]{1,0:T(8,128)(2,1)S(1)}, u32[]{:S(2)}, u32[]{:S(2)}) collective-permute-start(bf16[192,128]{1,0:T(8,128)(2,1)S(1)} %get-tuple-element.13.own), channel_id=1, source_target_pairs={{0,126},{1,127},{2,0},{3,1},{4,2},{5,3},{6,4},{7,5},{8,6},{9,7},{1... | collective-permute-start | bytes 147464 | tf_op jit(solution)/shard_map/ppermute | solution.py:467
  21.0 0.3 collective-permute-start.4
  21.3 8.1 %all-to-all-start = ((f32[128,1,128]{2,1,0:T(1,128)}), f32[128,1,128]{2,1,0:T(1,128)S(1)}, u32[]{:S(2)}, u32[]{:S(2)}) async-start(f32[128,1,128]{2,1,0:T(1,128)} %bitcast.8), calls=%async_computation | async-start | bytes 131072 | tf_op jit(solution)/shard_map/all_to_all | solution.py:470
  29.5 0.1 stack.23
  29.6 0.5 convert_element_type.11.kept
  30.1 20.5 %near_inner.1 = (f32[2,2,2,192,512]{4,3,2,1,0:T(8,128)}, bf16[16,512,512]{2,1,0:T(8,128)(2,1)}) custom-call(bf16[4,192,768]{2,1,0:T(8,128)(2,1)} %copy-done.3, bf16[4,192,768]{2,1,0:T(8,128)(2,1)} %copy-done.4, bf16[14,512,512]{2,1,0:T(8,128)(2,1)} %tables.2), custom_call_target="tpu_custom_call" | custom-call | flops 10000000000 | bytes 20000000 | tf_op jit(solution)/shard_map/near_inner/pallas_call | solution.py:225
  50.7 0.0 collective-permute-done.1.above
  50.7 0.0 collective-permute-done.below
  50.7 14.8 %near_outer.1.near = f32[2,2,2,192,512]{4,3,2,1,0:T(8,128)} custom-call(f32[5]{0:T(128)} %convert_element_type.11.kept, bf16[4,192,768]{2,1,0:T(8,128)(2,1)} %copy-done.3, bf16[4,192,768]{2,1,0:T(8,128)(2,1)} %copy-done.4, bf16[4,192,768]{2,1,0:T(8,128)(2,1)} %collective-permute-done.below, bf16[4,192,768]{2,1,0:T(8,128)(2,1)} %collective-permute-done.1.above, ...), custom_call_target="tpu_custom_call" | custom-call | flops 7000000000 | bytes 20000000 | tf_op jit(solution)/shard_map/near_outer/pallas_call | solution.py:257
  65.5 0.0 collective-permute-done.3.ahead2
  65.6 0.6 copy-done.7
  66.1 0.0 copy-done.8
  66.2 0.0 copy-done.9
  66.2 0.0 copy-done.6
  66.2 39.6 %transfer.1 = bf16[2,24,28,512]{3,2,1,0:T(8,128)(2,1)} custom-call(s32[1]{0:T(128)} %bitcast.parity, f32[5]{0:T(128)} %convert_element_type.11.kept, bf16[4,192,768]{2,1,0:T(8,128)(2,1)} %copy-done.3, bf16[4,192,768]{2,1,0:T(8,128)(2,1)} %collective-permute-done.below, bf16[4,192,768]{2,1,0:T(8,128)(2,1)} %collective-permute-done.1.above, ...), custom_call_target="tpu_custom_call" | custom-call | flops 12000000000 | bytes 20000000 | tf_op jit(solution)/shard_map/transfer/pallas_call | solution.py:435
  105.8 3.2 %copy.11 = bf16[2,24,28,512]{3,1,2,0:T(8,128)(2,1)} copy(bf16[2,24,28,512]{3,2,1,0:T(8,128)(2,1)} %transfer.1) | data formatting | bytes 2752512 | tf_op jit(solution)/shard_map/transfer/pallas_call | solution.py:435
  (21 shorter events, 0.1 us)
Async XLA Ops:
  0.0 2.8 %copy-start.1 = (bf16[8,128,128]{2,1,0:T(8,128)(2,1)S(1)}, bf16[8,128,128]{2,1,0:T(8,128)(2,1)}, u32[]{:S(2)}) copy-start(bf16[8,128,128]{2,1,0:T(8,128)(2,1)} %param.9) | copy-start | bytes 786436
  0.0 2.8 %copy-start.2 = (bf16[512,128]{1,0:T(8,128)(2,1)S(1)}, bf16[512,128]{1,0:T(8,128)(2,1)}, u32[]{:S(2)}) copy-start(bf16[512,128]{1,0:T(8,128)(2,1)} %anterpolate.3) | copy-start | bytes 393220
  2.8 47.9 %copy-start = (f32[192,128]{1,0:T(8,128)}, f32[192,128]{1,0:T(8,128)S(1)}, u32[]{:S(2)}) copy-start(f32[192,128]{1,0:T(8,128)S(1)} %broadcast_in_dim.8.mask) | copy-start | bytes 294916
  4.6 25.6 %copy-start.3 = (bf16[4,192,768]{2,1,0:T(8,128)(2,1)}, bf16[4,192,768]{2,1,0:T(8,128)(2,1)S(1)}, u32[]{:S(2)}) copy-start(bf16[4,192,768]{2,1,0:T(8,128)(2,1)S(1)} %get-tuple-element.11.low) | copy-start | bytes 3538948
  4.6 25.6 %copy-start.4 = (bf16[4,192,768]{2,1,0:T(8,128)(2,1)}, bf16[4,192,768]{2,1,0:T(8,128)(2,1)S(1)}, u32[]{:S(2)}) copy-start(bf16[4,192,768]{2,1,0:T(8,128)(2,1)S(1)} %get-tuple-element.12.high) | copy-start | bytes 3538948
  4.6 46.1 %copy-start.5 = (bf16[192,128]{1,0:T(8,128)(2,1)}, bf16[192,128]{1,0:T(8,128)(2,1)S(1)}, u32[]{:S(2)}) copy-start(bf16[192,128]{1,0:T(8,128)(2,1)S(1)} %get-tuple-element.13.own) | copy-start | bytes 147460
  4.6 46.1 %collective-permute-start.1 = (bf16[4,192,768]{2,1,0:T(8,128)(2,1)S(1)}, bf16[4,192,768]{2,1,0:T(8,128)(2,1)}, u32[]{:S(2)}, u32[]{:S(2)}) collective-permute-start(bf16[4,192,768]{2,1,0:T(8,128)(2,1)S(1)} %get-tuple-element.11.low), channel_id=1, source_target_pairs={{0,127},{1,0},{2,1},{3,2},{4,3},{5,4},{6,5},{7,6},{8,7},{9,8},{10,... | collective-permute-start | bytes 3538952 | tf_op jit(solution)/shard_map/ppermute | solution.py:465
  6.0 44.7 %collective-permute-start = (bf16[4,192,768]{2,1,0:T(8,128)(2,1)S(1)}, bf16[4,192,768]{2,1,0:T(8,128)(2,1)}, u32[]{:S(2)}, u32[]{:S(2)}) collective-permute-start(bf16[4,192,768]{2,1,0:T(8,128)(2,1)S(1)} %get-tuple-element.12.high), channel_id=1, source_target_pairs={{0,1},{1,2},{2,3},{3,4},{4,5},{5,6},{6,7},{7,8},{8,9},{9,10},{10,1... | collective-permute-start | bytes 3538952 | tf_op jit(solution)/shard_map/ppermute | solution.py:464
  7.4 58.2 %collective-permute-start.2 = (bf16[192,128]{1,0:T(8,128)(2,1)S(1)}, bf16[192,128]{1,0:T(8,128)(2,1)S(1)}, u32[]{:S(2)}, u32[]{:S(2)}) collective-permute-start(bf16[192,128]{1,0:T(8,128)(2,1)S(1)} %get-tuple-element.13.own), channel_id=1, source_target_pairs={{0,2},{1,3},{2,4},{3,5},{4,6},{5,7},{6,8},{7,9},{8,10},{9,11},{10,... | collective-permute-start | bytes 147464 | tf_op jit(solution)/shard_map/ppermute | solution.py:466
  8.7 56.9 %collective-permute-start.3 = (bf16[192,128]{1,0:T(8,128)(2,1)S(1)}, bf16[192,128]{1,0:T(8,128)(2,1)S(1)}, u32[]{:S(2)}, u32[]{:S(2)}) collective-permute-start(bf16[192,128]{1,0:T(8,128)(2,1)S(1)} %get-tuple-element.13.own), channel_id=1, source_target_pairs={{0,126},{1,127},{2,0},{3,1},{4,2},{5,3},{6,4},{7,5},{8,6},{9,7},{1... | collective-permute-start | bytes 147464 | tf_op jit(solution)/shard_map/ppermute | solution.py:467
  21.0 44.5 %collective-permute-start.4 = (bf16[192,128]{1,0:T(8,128)(2,1)S(1)}, bf16[192,128]{1,0:T(8,128)(2,1)S(1)}, u32[]{:S(2)}, u32[]{:S(2)}) collective-permute-start(bf16[192,128]{1,0:T(8,128)(2,1)S(1)} %get-tuple-element.13.own), channel_id=1, source_target_pairs={{0,3},{2,5},{4,7},{6,9},{8,11},{10,13},{12,15},{14,17},{16,19},{18... | collective-permute-start | bytes 147464 | tf_op jit(solution)/shard_map/ppermute | solution.py:469
  21.3 44.2 %all-to-all-start = ((f32[128,1,128]{2,1,0:T(1,128)}), f32[128,1,128]{2,1,0:T(1,128)S(1)}, u32[]{:S(2)}, u32[]{:S(2)}) async-start(f32[128,1,128]{2,1,0:T(1,128)} %bitcast.8), calls=%async_computation | async-start | bytes 131072 | tf_op jit(solution)/shard_map/all_to_all | solution.py:470
  65.5 0.6 copy-start.7
  65.5 0.6 copy-start.8
  65.5 0.6 copy-start.9
  65.6 0.6 copy-start.6
where the time goes:
time: 109 us
  Pallas kernels  76.7 us (70%)
  starting transfers between devices  24.9 us (23%)
  local copies, waits for them, and re-layouts  5.99 us (5%)
  other arithmetic  1.29 us (1%)
    pallas_call x1, Pallas kernels, transfer(): pl.pallas_call(transfer_kernel, name='transfer', out_shape=jax.ShapeDtype...  39.6 us
    pallas_call x1, Pallas kernels, near_inner(): pl.pallas_call(near_inner_kernel, name='near_inner', out_shape=(jax.Shape...  20.5 us
    pallas_call x1, Pallas kernels, near_outer(): pl.pallas_call(near_outer_kernel, name='near_outer', out_shape=jax.ShapeD...  14.8 us
    ppermute x1, starting transfers between devices, body(): ahead2 = lax.ppermute(own, 'leaf', around(count, -2))  12.3 us
    all_to_all x1, starting transfers between devices, body(): charge = lax.all_to_all(partial, 'leaf', 0, 0, tiled=True)  8.1 us
    pallas_call x1, local copies, waits for them, and re-layouts, transfer(): pl.pallas_call(transfer_kernel, name='transfer', out_shape=jax.ShapeDtype...  3.24 us
    unnamed x22, local copies, waits for them, and re-layouts  2.47 us
  transfers between devices with their start and end apart: 6, of which 0 were waited for; matrix products, arithmetic and copies ran while one was open for 1% of the time, Pallas kernels for 32%

commit v1 on v0

--- a/solution.py
+++ b/solution.py
@@ -16,6 +16,7 @@
 COARSE = 48
 VMEM = pl.BlockSpec(memory_space=pltpu.VMEM)
 SMEM = pl.BlockSpec(memory_space=pltpu.SMEM)
+ANY = pl.BlockSpec(memory_space=pl.ANY)
 
 
 def mul(a, b):
@@ -198,11 +199,19 @@
                 held[1, px] -= value
 
 
-def near_inner_kernel(low, high, tables, near, outer, parts, inner, held, made):
-    outer_weights(tables, outer)
-    inner_weights(tables, outer, inner)
+def near_inner_kernel(low, high, tables_in, near, outer_out, parts, inner, held, made, tables, outer, sems):
+    ends = pltpu.make_async_copy(tables_in.at[5:14], tables.at[5:14], sems.at[0])
+    flats = pltpu.make_async_copy(tables_in.at[0:5], tables.at[0:5], sems.at[1])
+    ends.start()
+    flats.start()
     spread(low, high, lambda d1, d2: d1 + d2, parts, 0)
     spread(low, high, lambda d1, d2: d2 - d1, parts, 16)
+    ends.wait()
+    outer_weights(tables, outer)
+    leaving = pltpu.make_async_copy(outer, outer_out, sems.at[2])
+    leaving.start()
+    flats.wait()
+    inner_weights(tables, outer, inner)
 
     def product(a):
         def one(b, c):
@@ -219,6 +228,7 @@
     gathered_products(product(1), held, made)
     near[0] += held[...]
     near[1] -= held[...]
+    leaving.wait()
 
 
 def near_inner(low, high, tables):
@@ -229,28 +239,37 @@
             jax.ShapeDtypeStruct((2, 2, 2, ROWS, PTS), F32),
             jax.ShapeDtypeStruct((16, PTS, PTS), BF16),
         ),
-        in_specs=[VMEM] * 3,
-        out_specs=(VMEM,) * 2,
+        in_specs=[VMEM, VMEM, ANY],
+        out_specs=(VMEM, ANY),
         scratch_shapes=[
             pltpu.VMEM((32, ROWS, PTS), BF16),
             pltpu.VMEM((20, PTS, PTS), BF16),
             pltpu.VMEM((2, 2, ROWS, PTS), F32),
             pltpu.VMEM((4, ROWS, PTS), F32),
+            pltpu.VMEM((14, PTS, PTS), BF16),
+            pltpu.VMEM((16, PTS, PTS), BF16),
+            pltpu.SemaphoreType.DMA((3,)),
         ],
         cost_estimate=pl.CostEstimate(flops=10_000_000_000, bytes_accessed=20_000_000, transcendentals=0),
         compiler_params=pltpu.CompilerParams(vmem_limit_bytes=60 << 20),
     )(low, high, tables)
 
 
-def near_outer_kernel(kept, low, high, below, above, outer, near_in, near, parts, held, made):
+def near_outer_kernel(kept, low, high, below, above, outer_in, near_in, near, parts, held, made, outer, sems):
+    weights = pltpu.make_async_copy(outer_in, outer, sems.at[0])
+    inner_part = pltpu.make_async_copy(near_in, near, sems.at[1])
+    weights.start()
+    inner_part.start()
     spread(below, high, lambda d0, d2: d0 * kept[0] - d2, parts, 0)
     spread(low, above, lambda d1, d3: d1 - d3 * kept[1], parts, 16)
+    weights.wait()
     gathered_products(
         lambda b, c: mul_t(parts[b * 4 + c], outer[MIRROR[b] * 4 + MIRROR[c]]), held, made
     )
-    near[0] = near_in[0] + held[...]
+    inner_part.wait()
+    near[0] += held[...]
     gathered_products(lambda b, c: mul(parts[16 + b * 4 + c], outer[b * 4 + c]), held, made)
-    near[1] = near_in[1] - held[...]
+    near[1] -= held[...]
 
 
 def near_outer(kept, low, high, below, above, outer, near):
@@ -258,12 +277,14 @@
         near_outer_kernel,
         name="near_outer",
         out_shape=jax.ShapeDtypeStruct((2, 2, 2, ROWS, PTS), F32),
-        in_specs=[SMEM] + [VMEM] * 6,
+        in_specs=[SMEM] + [VMEM] * 4 + [ANY] * 2,
         out_specs=VMEM,
         scratch_shapes=[
             pltpu.VMEM((32, ROWS, PTS), BF16),
             pltpu.VMEM((2, 2, ROWS, PTS), F32),
             pltpu.VMEM((4, ROWS, PTS), F32),
+            pltpu.VMEM((16, PTS, PTS), BF16),
+            pltpu.SemaphoreType.DMA((2,)),
         ],
         cost_estimate=pl.CostEstimate(flops=7_000_000_000, bytes_accessed=20_000_000, transcendentals=0),
         compiler_params=pltpu.CompilerParams(vmem_limit_bytes=60 << 20),
@@ -351,9 +372,13 @@
 
 
 def transfer_kernel(
-    parity, kept, low, below, above, own, back2, ahead2, far3, mask, charge, merge, anterpolate, tables, near,
-    potential, leaves, lines, stage, weave, coarse,
+    parity, kept, low, below, above, own, back2, ahead2, far3, mask, charge, merge, anterpolate, tables_in, near_in,
+    potential, leaves, lines, stage, weave, coarse, tables, near, fine, sems,
 ):
+    operators = pltpu.make_async_copy(tables_in, tables, sems.at[0])
+    near_part = pltpu.make_async_copy(near_in, near, sems.at[1])
+    operators.start()
+    near_part.start()
     packs = (below, below, low, low, above, above)
     leaves[...] = jnp.zeros_like(leaves)
     for n in range(6):
@@ -371,6 +396,7 @@
         coarse_lines(box if flag is None else box * kept[flag], stage, n + side, lines)
     coarse_lines(far3[...].astype(F32) * kept[4], stage, 5 - 5 * side, lines)
 
+    operators.wait()
     for pz in range(2):
 
         @pl.when(side == pz)
@@ -400,23 +426,26 @@
     leaf_count = 2.0 * 24 * 28 * 128
     factor = wide(mask[...] * (leaf_count * PTS / total_charge))
 
+    for py in range(2):
+        for pz in range(2):
+            first = (4 * pz + 2 * py) * K
+            fine[pz * 2 + py] = mul_t(parent_local, merge[first : first + 2 * K, :])
+        for dz in range(-3, 4):
+            layers = [pz for pz in range(2) if -2 <= dz + pz <= 3]
+
+            def source(jy, jx):
+                lines_here = pl.ds(GROUP * (1 + jy // 2), ROWS)
+                here = [leaves[dz + pz + 2, jy % 2, lines_here, (jx + 2) * K : (jx + 3) * K] for pz in layers]
+                return jnp.concatenate(here, axis=0)
+
+            for term in transfer_terms(tables, dz, range(-2, 4), py, source):
+                for n, pz in enumerate(layers):
+                    fine[pz * 2 + py] += term[n * ROWS : n * ROWS + ROWS]
+
+    near_part.wait()
     for pz in range(2):
         for py in range(2):
-            total = mul_t(parent_local, merge[(4 * pz + 2 * py) * K : (4 * pz + 2 * py) * K + 2 * K, :])
-            for jz in range(-2, 4):
-                for term in transfer_terms(
-                    tables,
-                    jz - pz,
-                    range(-2, 4),
-                    py,
-                    lambda jy, jx: leaves[
-                        jz + 2,
-                        jy % 2,
-                        GROUP * (1 + jy // 2) : GROUP * (1 + jy // 2) + ROWS,
-                        (jx + 2) * K : (jx + 3) * K,
-                    ],
-                ):
-                    total = total + term
+            total = fine[pz * 2 + py]
             local = total.astype(BF16)
             for px in range(2):
                 far = mul_t(local[:, px * K : px * K + K], anterpolate[...])
@@ -436,7 +465,7 @@
         transfer_kernel,
         name="transfer",
         out_shape=jax.ShapeDtypeStruct((2, 2 * LINES, 28, PTS), BF16),
-        in_specs=[SMEM] * 2 + [VMEM] * 13,
+        in_specs=[SMEM] * 2 + [VMEM] * 11 + [ANY] * 2,
         out_specs=VMEM,
         scratch_shapes=[
             pltpu.VMEM((6, 2, ROWS + 2 * GROUP, 6 * K), BF16),
@@ -444,6 +473,10 @@
             pltpu.VMEM((ROWS, K), F32),
             pltpu.VMEM((LINES * 4, 32, 128), F32),
             pltpu.VMEM((2, COARSE, 2 * K), F32),
+            pltpu.VMEM((len(RANK), K, K), BF16),
+            pltpu.VMEM((2, 2, 2, ROWS, PTS), F32),
+            pltpu.VMEM((4, ROWS, 2 * K), F32),
+            pltpu.SemaphoreType.DMA((2,)),
         ],
         cost_estimate=pl.CostEstimate(flops=12_000_000_000, bytes_accessed=20_000_000, transcendentals=0),
         compiler_params=pltpu.CompilerParams(vmem_limit_bytes=60 << 20),
@@ -467,13 +500,14 @@
     ahead2 = lax.ppermute(own, "leaf", around(count, -2))
     crossed = [(i, (i + 3) % count) for i in range(0, count, 2)]
     far3 = lax.ppermute(own, "leaf", crossed + [(j, i) for i, j in crossed])
-    charge = lax.all_to_all(partial, "leaf", 0, 0, tiled=True)
     parity = place % 2
     source3 = place + 3 - 6 * parity
     kept = jnp.stack(
         [place >= 1, place < count - 1, place >= 2, place < count - 2, (source3 >= 0) & (source3 < count)]
     ).astype(F32)
     near, outer = near_inner(low, high, near_tables)
+    partial, near = lax.optimization_barrier((partial, near))
+    charge = lax.all_to_all(partial, "leaf", 0, 0, tiled=True)
     near = near_outer(kept, low, high, below, above, outer, near)
     return transfer(
         parity.reshape(1), kept, low, below, above, own, back2, ahead2, far3, mask, charge, merge, anterpolate,

time: 109 us -> 89.3 us (0.82)
  Pallas kernels: 76.7 us -> 56.7 us
    pallas_call x1, Pallas kernels: 39.6 us -> 24 us  [transfer(): pl.pallas_call(transfer_kernel, name='transfer', out_shape=jax.ShapeDtype...]
    pallas_call x1, Pallas kernels: 14.8 us -> 12.5 us  [near_outer(): pl.pallas_call(near_outer_kernel, name='near_outer', out_shape=jax.ShapeD...]
    pallas_call x1, Pallas kernels: 20.5 us -> 18.4 us  [near_inner(): pl.pallas_call(near_inner_kernel, name='near_inner', out_shape=(jax.Shape...]
  transfers between devices with their start and end apart: 6 -> 6, of which waited for: 0 -> 0; matrix products, arithmetic and copies ran while one was open for 1% -> 1% of each run, Pallas kernels for 32% -> 35%
where the time goes in v1:
time: 89.3 us; the launch traced here: 89 us
  Pallas kernels  56.7 us (63%)
  starting transfers between devices  24.9 us (28%)
  local copies, waits for them, and re-layouts  5.99 us (7%)
  other arithmetic  1.29 us (1%)
    pallas_call x1, Pallas kernels, transfer(): pl.pallas_call(transfer_kernel, name='transfer', out_shape=jax.ShapeDtype...  24 us
    pallas_call x1, Pallas kernels, near_inner(): pl.pallas_call(near_inner_kernel, name='near_inner', out_shape=(jax.Shape...  18.4 us
    pallas_call x1, Pallas kernels, near_outer(): pl.pallas_call(near_outer_kernel, name='near_outer', out_shape=jax.ShapeD...  12.5 us
    ppermute x1, starting transfers between devices, body(): ahead2 = lax.ppermute(own, 'leaf', around(count, -2))  12.3 us
    all_to_all x1, starting transfers between devices, body(): charge = lax.all_to_all(partial, 'leaf', 0, 0, tiled=True)  8.1 us
    pallas_call x1, local copies, waits for them, and re-layouts, transfer(): pl.pallas_call(transfer_kernel, name='transfer', out_shape=jax.ShapeDtype...  3.24 us
    unnamed x22, local copies, waits for them, and re-layouts  2.47 us
    pallas_call x1, Pallas kernels, prologue(): pl.pallas_call(prologue_kernel, name='prologue', out_shape=(pack, pack, j...  1.79 us
  transfers between devices with their start and end apart: 6, of which 0 were waited for; matrix products, arithmetic and copies ran while one was open for 1% of the time, Pallas kernels for 35%

profile of v1, /device:TPU:1, one launch (start us, length us, event | category | flops | bytes accessed | tf_op | source)
XLA Modules:
  0.0 89.0 jit_solution(6109357479708688333)
XLA Ops:
  0.0 0.7 convert_element_type.12
  0.8 0.1 broadcast_in_dim.7
  0.8 1.8 %copy.9.density = bf16[2,24,28,512]{3,2,1,0:T(8,128)(2,1)S(1)} copy(bf16[2,24,28,512]{3,1,2,0:T(8,128)(2,1)} %param.6) | data formatting | bytes 2752512 | tf_op args[0]
  2.7 0.1 broadcast_in_dim.8.mask
  2.8 1.8 %prologue.1 = (bf16[4,192,768]{2,1,0:T(8,128)(2,1)S(1)}, bf16[4,192,768]{2,1,0:T(8,128)(2,1)S(1)}, bf16[192,128]{1,0:T(8,128)(2,1)S(1)}, f32[128,128]{1,0:T(8,128)}) custom-call(bf16[2,24,28,512]{3,2,1,0:T(8,128)(2,1)S(1)} %copy.9.density, f32[192,128]{1,0:T(8,128)S(1)} %broadcast_in_dim.8.mask, bf16[512,128]{1,0:T(8,128)(2,1)S(1)} %copy-done.2, ...), custom_call_target="tpu_custom_call" | custom-call | tf_op jit(solution)/shard_map/prologue/pallas_call | solution.py:73
  4.6 1.4 %collective-permute-start.1 = (bf16[4,192,768]{2,1,0:T(8,128)(2,1)S(1)}, bf16[4,192,768]{2,1,0:T(8,128)(2,1)}, u32[]{:S(2)}, u32[]{:S(2)}) collective-permute-start(bf16[4,192,768]{2,1,0:T(8,128)(2,1)S(1)} %get-tuple-element.13.low), channel_id=1, source_target_pairs={{0,127},{1,0},{2,1},{3,2},{4,3},{5,4},{6,5},{7,6},{8,7},{9,8},{10,... | collective-permute-start | bytes 3538952 | tf_op jit(solution)/shard_map/ppermute | solution.py:498
  6.0 1.3 %collective-permute-start = (bf16[4,192,768]{2,1,0:T(8,128)(2,1)S(1)}, bf16[4,192,768]{2,1,0:T(8,128)(2,1)}, u32[]{:S(2)}, u32[]{:S(2)}) collective-permute-start(bf16[4,192,768]{2,1,0:T(8,128)(2,1)S(1)} %get-tuple-element.14.high), channel_id=1, source_target_pairs={{0,1},{1,2},{2,3},{3,4},{4,5},{5,6},{6,7},{7,8},{8,9},{9,10},{10,1... | collective-permute-start | bytes 3538952 | tf_op jit(solution)/shard_map/ppermute | solution.py:497
  7.4 1.3 %collective-permute-start.2 = (bf16[192,128]{1,0:T(8,128)(2,1)S(1)}, bf16[192,128]{1,0:T(8,128)(2,1)S(1)}, u32[]{:S(2)}, u32[]{:S(2)}) collective-permute-start(bf16[192,128]{1,0:T(8,128)(2,1)S(1)} %get-tuple-element.15.own), channel_id=1, source_target_pairs={{0,2},{1,3},{2,4},{3,5},{4,6},{5,7},{6,8},{7,9},{8,10},{9,11},{10,... | collective-permute-start | bytes 147464 | tf_op jit(solution)/shard_map/ppermute | solution.py:499
  8.7 12.3 %collective-permute-start.3 = (bf16[192,128]{1,0:T(8,128)(2,1)S(1)}, bf16[192,128]{1,0:T(8,128)(2,1)S(1)}, u32[]{:S(2)}, u32[]{:S(2)}) collective-permute-start(bf16[192,128]{1,0:T(8,128)(2,1)S(1)} %get-tuple-element.15.own), channel_id=1, source_target_pairs={{0,126},{1,127},{2,0},{3,1},{4,2},{5,3},{6,4},{7,5},{8,6},{9,7},{1... | collective-permute-start | bytes 147464 | tf_op jit(solution)/shard_map/ppermute | solution.py:500
  21.0 0.3 collective-permute-start.4
  21.4 18.4 %near_inner.1 = (f32[2,2,2,192,512]{4,3,2,1,0:T(8,128)}, bf16[16,512,512]{2,1,0:T(8,128)(2,1)}) custom-call(bf16[4,192,768]{2,1,0:T(8,128)(2,1)} %copy-done.3, bf16[4,192,768]{2,1,0:T(8,128)(2,1)} %copy-done.4, bf16[14,512,512]{2,1,0:T(8,128)(2,1)} %tables_in.2), custom_call_target="tpu_custom_call" | custom-call | flops 10000000000 | bytes 20000000 | tf_op jit(solution)/shard_map/near_inner/pallas_call | solution.py:235
  39.8 8.1 %all-to-all-start = ((f32[128,1,128]{2,1,0:T(1,128)}), f32[128,1,128]{2,1,0:T(1,128)S(1)}, u32[]{:S(2)}, u32[]{:S(2)}) async-start(f32[128,1,128]{2,1,0:T(1,128)} %bitcast.8), calls=%async_computation | async-start | bytes 131072 | tf_op jit(solution)/shard_map/all_to_all | solution.py:510
  47.9 0.1 stack.23
  48.0 0.5 convert_element_type.11.kept
  48.6 0.0 collective-permute-done.1.above
  48.6 12.5 %near_outer.1.near_in = f32[2,2,2,192,512]{4,3,2,1,0:T(8,128)} custom-call(f32[5]{0:T(128)} %convert_element_type.11.kept, bf16[4,192,768]{2,1,0:T(8,128)(2,1)} %copy-done.3, bf16[4,192,768]{2,1,0:T(8,128)(2,1)} %copy-done.4, bf16[4,192,768]{2,1,0:T(8,128)(2,1)} %collective-permute-done.below, bf16[4,192,768]{2,1,0:T(8,128)(2,1)} %collective-permute-done.1.above, ...), custom_call_target="tpu_custom_call" | custom-call | flops 7000000000 | bytes 20000000 | tf_op jit(solution)/shard_map/near_outer/pallas_call | solution.py:276
  61.1 0.0 collective-permute-done.2.back2
  61.2 0.0 all-to-all-done
  61.2 0.5 copy-done.7
  61.8 0.0 copy-done.8
  61.8 0.0 copy-done.9
  61.8 0.0 copy-done.6
  61.8 24.0 %transfer.1 = bf16[2,24,28,512]{3,2,1,0:T(8,128)(2,1)} custom-call(s32[1]{0:T(128)} %bitcast.parity, f32[5]{0:T(128)} %convert_element_type.11.kept, bf16[4,192,768]{2,1,0:T(8,128)(2,1)} %copy-done.3, bf16[4,192,768]{2,1,0:T(8,128)(2,1)} %collective-permute-done.below, bf16[4,192,768]{2,1,0:T(8,128)(2,1)} %collective-permute-done.1.above, ...), custom_call_target="tpu_custom_call" | custom-call | flops 12000000000 | bytes 20000000 | tf_op jit(solution)/shard_map/transfer/pallas_call | solution.py:464
  85.8 3.2 %copy.11 = bf16[2,24,28,512]{3,1,2,0:T(8,128)(2,1)} copy(bf16[2,24,28,512]{3,2,1,0:T(8,128)(2,1)} %transfer.1) | data formatting | bytes 2752512 | tf_op jit(solution)/shard_map/transfer/pallas_call | solution.py:464
  (21 shorter events, 0.1 us)
Async XLA Ops:
  0.0 2.8 %copy-start.1 = (bf16[8,128,128]{2,1,0:T(8,128)(2,1)S(1)}, bf16[8,128,128]{2,1,0:T(8,128)(2,1)}, u32[]{:S(2)}) copy-start(bf16[8,128,128]{2,1,0:T(8,128)(2,1)} %param.9) | copy-start | bytes 786436
  0.0 2.8 %copy-start.2 = (bf16[512,128]{1,0:T(8,128)(2,1)S(1)}, bf16[512,128]{1,0:T(8,128)(2,1)}, u32[]{:S(2)}) copy-start(bf16[512,128]{1,0:T(8,128)(2,1)} %anterpolate.3) | copy-start | bytes 393220
  2.8 37.0 %copy-start = (f32[192,128]{1,0:T(8,128)}, f32[192,128]{1,0:T(8,128)S(1)}, u32[]{:S(2)}) copy-start(f32[192,128]{1,0:T(8,128)S(1)} %broadcast_in_dim.8.mask) | copy-start | bytes 294916
  4.6 16.8 %copy-start.3 = (bf16[4,192,768]{2,1,0:T(8,128)(2,1)}, bf16[4,192,768]{2,1,0:T(8,128)(2,1)S(1)}, u32[]{:S(2)}) copy-start(bf16[4,192,768]{2,1,0:T(8,128)(2,1)S(1)} %get-tuple-element.13.low) | copy-start | bytes 3538948
  4.6 16.8 %copy-start.4 = (bf16[4,192,768]{2,1,0:T(8,128)(2,1)}, bf16[4,192,768]{2,1,0:T(8,128)(2,1)S(1)}, u32[]{:S(2)}) copy-start(bf16[4,192,768]{2,1,0:T(8,128)(2,1)S(1)} %get-tuple-element.14.high) | copy-start | bytes 3538948
  4.6 35.2 %copy-start.5 = (bf16[192,128]{1,0:T(8,128)(2,1)}, bf16[192,128]{1,0:T(8,128)(2,1)S(1)}, u32[]{:S(2)}) copy-start(bf16[192,128]{1,0:T(8,128)(2,1)S(1)} %get-tuple-element.15.own) | copy-start | bytes 147460
  4.6 44.0 %collective-permute-start.1 = (bf16[4,192,768]{2,1,0:T(8,128)(2,1)S(1)}, bf16[4,192,768]{2,1,0:T(8,128)(2,1)}, u32[]{:S(2)}, u32[]{:S(2)}) collective-permute-start(bf16[4,192,768]{2,1,0:T(8,128)(2,1)S(1)} %get-tuple-element.13.low), channel_id=1, source_target_pairs={{0,127},{1,0},{2,1},{3,2},{4,3},{5,4},{6,5},{7,6},{8,7},{9,8},{10,... | collective-permute-start | bytes 3538952 | tf_op jit(solution)/shard_map/ppermute | solution.py:498
  6.0 42.6 %collective-permute-start = (bf16[4,192,768]{2,1,0:T(8,128)(2,1)S(1)}, bf16[4,192,768]{2,1,0:T(8,128)(2,1)}, u32[]{:S(2)}, u32[]{:S(2)}) collective-permute-start(bf16[4,192,768]{2,1,0:T(8,128)(2,1)S(1)} %get-tuple-element.14.high), channel_id=1, source_target_pairs={{0,1},{1,2},{2,3},{3,4},{4,5},{5,6},{6,7},{7,8},{8,9},{9,10},{10,1... | collective-permute-start | bytes 3538952 | tf_op jit(solution)/shard_map/ppermute | solution.py:497
  7.4 53.8 %collective-permute-start.2 = (bf16[192,128]{1,0:T(8,128)(2,1)S(1)}, bf16[192,128]{1,0:T(8,128)(2,1)S(1)}, u32[]{:S(2)}, u32[]{:S(2)}) collective-permute-start(bf16[192,128]{1,0:T(8,128)(2,1)S(1)} %get-tuple-element.15.own), channel_id=1, source_target_pairs={{0,2},{1,3},{2,4},{3,5},{4,6},{5,7},{6,8},{7,9},{8,10},{9,11},{10,... | collective-permute-start | bytes 147464 | tf_op jit(solution)/shard_map/ppermute | solution.py:499
  8.7 52.5 %collective-permute-start.3 = (bf16[192,128]{1,0:T(8,128)(2,1)S(1)}, bf16[192,128]{1,0:T(8,128)(2,1)S(1)}, u32[]{:S(2)}, u32[]{:S(2)}) collective-permute-start(bf16[192,128]{1,0:T(8,128)(2,1)S(1)} %get-tuple-element.15.own), channel_id=1, source_target_pairs={{0,126},{1,127},{2,0},{3,1},{4,2},{5,3},{6,4},{7,5},{8,6},{9,7},{1... | collective-permute-start | bytes 147464 | tf_op jit(solution)/shard_map/ppermute | solution.py:500
  21.0 40.2 %collective-permute-start.4 = (bf16[192,128]{1,0:T(8,128)(2,1)S(1)}, bf16[192,128]{1,0:T(8,128)(2,1)S(1)}, u32[]{:S(2)}, u32[]{:S(2)}) collective-permute-start(bf16[192,128]{1,0:T(8,128)(2,1)S(1)} %get-tuple-element.15.own), channel_id=1, source_target_pairs={{0,3},{2,5},{4,7},{6,9},{8,11},{10,13},{12,15},{14,17},{16,19},{18... | collective-permute-start | bytes 147464 | tf_op jit(solution)/shard_map/ppermute | solution.py:502
  39.8 21.4 %all-to-all-start = ((f32[128,1,128]{2,1,0:T(1,128)}), f32[128,1,128]{2,1,0:T(1,128)S(1)}, u32[]{:S(2)}, u32[]{:S(2)}) async-start(f32[128,1,128]{2,1,0:T(1,128)} %bitcast.8), calls=%async_computation | async-start | bytes 131072 | tf_op jit(solution)/shard_map/all_to_all | solution.py:510
  61.1 0.6 copy-start.7
  61.2 0.6 copy-start.8
  61.2 0.6 copy-start.9
  61.2 0.6 copy-start.6

commit v2 on v1

--- a/solution.py
+++ b/solution.py
@@ -116,7 +116,7 @@
         here = pl.ds(pl.multiple_of((n // 4) * 128, 128), 128)
         there = pl.ds(pl.multiple_of((n % 4) * 128, 128), 128)
         t = [tables[m, here, there].astype(F32) for m in range(5)]
-        f = [None] + [tables[m, there, here].astype(F32).T for m in range(1, 5)]
+        f = [None] + [tables[m, there, here].T.astype(F32) for m in range(1, 5)]
         above = taps(t[2], t[3], t[4])
         below = taps(f[4], f[3], f[2])
         level = taps(f[1], t[0], t[1])
@@ -128,7 +128,7 @@
             else:
                 flat = 0.5 * (below[c] + above[c] - level[c])
             ends = outer[b * 4 + c, here, there].astype(F32)
-            ends = ends + outer[MIRROR[b] * 4 + MIRROR[c], there, here].astype(F32).T
+            ends = ends + outer[MIRROR[b] * 4 + MIRROR[c], there, here].T.astype(F32)
             inner[k, here, there] = (0.5 * (ends + flat)).astype(BF16)
             inner[10 + k, here, there] = (0.5 * (ends - flat)).astype(BF16)
         return 0
@@ -373,7 +373,7 @@
 
 def transfer_kernel(
     parity, kept, low, below, above, own, back2, ahead2, far3, mask, charge, merge, anterpolate, tables_in, near_in,
-    potential, leaves, lines, stage, weave, coarse, tables, near, fine, sems,
+    potential, leaves, lines, stage, weave, flat, coarse, tables, near, fine, sems,
 ):
     operators = pltpu.make_async_copy(tables_in, tables, sems.at[0])
     near_part = pltpu.make_async_copy(near_in, near, sems.at[1])
@@ -450,28 +450,29 @@
             for px in range(2):
                 far = mul_t(local[:, px * K : px * K + K], anterpolate[...])
                 found = (near[pz, py, px] + far) * factor
-                for yp in range(LINES):
+                for h in range(4):
+                    flat[px, h] = found[:, h * 128 : h * 128 + 128]
+                for xp in range(14):
                     for h in range(4):
-                        weave[yp * 4 + h, pl.ds(px, GROUP, stride=2), :] = found[
-                            yp * GROUP : yp * GROUP + GROUP, h * 128 : h * 128 + 128
-                        ]
-            for yp in range(LINES):
-                for h in range(4):
-                    potential[pz, 2 * yp + py, :, h * 128 : h * 128 + 128] = weave[yp * 4 + h, 0:28, :].astype(BF16)
+                        weave[h, 2 * xp + px, pl.ds(py, LINES, stride=2), :] = flat[px, h, pl.ds(xp, LINES, stride=GROUP), :]
+        for x in range(28):
+            for h in range(4):
+                potential[pz, x, :, h * 128 : h * 128 + 128] = weave[h, x].astype(BF16)
 
 
 def transfer(parity, kept, low, below, above, own, back2, ahead2, far3, mask, charge, merge, anterpolate, tables, near):
     return pl.pallas_call(
         transfer_kernel,
         name="transfer",
-        out_shape=jax.ShapeDtypeStruct((2, 2 * LINES, 28, PTS), BF16),
+        out_shape=jax.ShapeDtypeStruct((2, 28, 2 * LINES, PTS), BF16),
         in_specs=[SMEM] * 2 + [VMEM] * 11 + [ANY] * 2,
         out_specs=VMEM,
         scratch_shapes=[
             pltpu.VMEM((6, 2, ROWS + 2 * GROUP, 6 * K), BF16),
             pltpu.VMEM((6, 6, COARSE, 6 * K), BF16),
             pltpu.VMEM((ROWS, K), F32),
-            pltpu.VMEM((LINES * 4, 32, 128), F32),
+            pltpu.VMEM((4, 28, 2 * LINES, 128), F32),
+            pltpu.VMEM((2, 4, ROWS, 128), F32),
             pltpu.VMEM((2, COARSE, 2 * K), F32),
             pltpu.VMEM((len(RANK), K, K), BF16),
             pltpu.VMEM((2, 2, 2, ROWS, PTS), F32),
@@ -496,23 +497,24 @@
     place = lax.axis_index("leaf")
     below = lax.ppermute(high, "leaf", around(count, 1))
     above = lax.ppermute(low, "leaf", around(count, -1))
-    back2 = lax.ppermute(own, "leaf", around(count, 2))
-    ahead2 = lax.ppermute(own, "leaf", around(count, -2))
-    crossed = [(i, (i + 3) % count) for i in range(0, count, 2)]
-    far3 = lax.ppermute(own, "leaf", crossed + [(j, i) for i, j in crossed])
     parity = place % 2
     source3 = place + 3 - 6 * parity
     kept = jnp.stack(
         [place >= 1, place < count - 1, place >= 2, place < count - 2, (source3 >= 0) & (source3 < count)]
     ).astype(F32)
     near, outer = near_inner(low, high, near_tables)
-    partial, near = lax.optimization_barrier((partial, near))
+    partial, own, near = lax.optimization_barrier((partial, own, near))
     charge = lax.all_to_all(partial, "leaf", 0, 0, tiled=True)
+    back2 = lax.ppermute(own, "leaf", around(count, 2))
+    ahead2 = lax.ppermute(own, "leaf", around(count, -2))
+    crossed = [(i, (i + 3) % count) for i in range(0, count, 2)]
+    far3 = lax.ppermute(own, "leaf", crossed + [(j, i) for i, j in crossed])
     near = near_outer(kept, low, high, below, above, outer, near)
-    return transfer(
+    potential = transfer(
         parity.reshape(1), kept, low, below, above, own, back2, ahead2, far3, mask, charge, merge, anterpolate,
         transfer_tables, near,
     )
+    return jnp.swapaxes(potential, 1, 2)
 
 
 def solution(mesh):

time: 89.3 us -> 82.2 us (0.920)
  starting transfers between devices: 24.9 us -> 20.4 us
  local copies, waits for them, and re-layouts: 5.99 us -> 2.75 us
    ppermute x1, starting transfers between devices: 12.3 us -> 0.46 us  [body(): ahead2 = lax.ppermute(own, 'leaf', around(count, -2))]
    ppermute x1, starting transfers between devices: 0.34 us -> 8.92 us  [body(): far3 = lax.ppermute(own, 'leaf', crossed + [(j, i) for i, j in crossed])]
    pallas_call x1 -> x0, local copies, waits for them, and re-layouts: 3.24 us -> none  [transfer(): pl.pallas_call(transfer_kernel, name='transfer', out_shape=jax.ShapeDtype...]
    ppermute x1, starting transfers between devices: 1.42 us -> 0.01 us  [body(): above = lax.ppermute(low, 'leaf', around(count, -1))]
    ppermute x1, starting transfers between devices: 1.34 us -> 2.69 us  [body(): below = lax.ppermute(high, 'leaf', around(count, 1))]
    pallas_call x1, Pallas kernels: 24 us -> 24.9 us  [transfer(): pl.pallas_call(transfer_kernel, name='transfer', out_shape=jax.ShapeDtype...]
  transfers between devices with their start and end apart: 6 -> 6, of which waited for: 0 -> 0; matrix products, arithmetic and copies ran while one was open for 1% -> 1% of each run, Pallas kernels for 35% -> 37%
where the time goes in v2:
time: 82.2 us; the launch traced here: 82 us
  Pallas kernels  57.2 us (70%)
  starting transfers between devices  20.4 us (25%)
  local copies, waits for them, and re-layouts  2.75 us (3%)
  other arithmetic  1.29 us (2%)
    pallas_call x1, Pallas kernels, transfer(): pl.pallas_call(transfer_kernel, name='transfer', out_shape=jax.ShapeDtype...  24.9 us
    pallas_call x1, Pallas kernels, near_inner(): pl.pallas_call(near_inner_kernel, name='near_inner', out_shape=(jax.Shape...  18 us
    pallas_call x1, Pallas kernels, near_outer(): pl.pallas_call(near_outer_kernel, name='near_outer', out_shape=jax.ShapeD...  12.5 us
    ppermute x1, starting transfers between devices, body(): far3 = lax.ppermute(own, 'leaf', crossed + [(j, i) for i, j in crossed])  8.92 us
    all_to_all x1, starting transfers between devices, body(): charge = lax.all_to_all(partial, 'leaf', 0, 0, tiled=True)  7.34 us
    ppermute x1, starting transfers between devices, body(): below = lax.ppermute(high, 'leaf', around(count, 1))  2.69 us
    unnamed x22, local copies, waits for them, and re-layouts  2.48 us
    pallas_call x1, Pallas kernels, prologue(): pl.pallas_call(prologue_kernel, name='prologue', out_shape=(pack, pack, j...  1.79 us
  transfers between devices with their start and end apart: 6, of which 0 were waited for; matrix products, arithmetic and copies ran while one was open for 1% of the time, Pallas kernels for 37%

profile of v2, /device:TPU:1, one launch (start us, length us, event | category | flops | bytes accessed | tf_op | source)
XLA Modules:
  0.0 82.0 jit_solution(15216913201981014975)
XLA Ops:
  0.0 0.7 convert_element_type.12
  0.8 0.1 broadcast_in_dim.7
  0.8 1.8 %copy.8.density = bf16[2,24,28,512]{3,2,1,0:T(8,128)(2,1)S(1)} copy(bf16[2,24,28,512]{3,1,2,0:T(8,128)(2,1)} %param.6) | data formatting | bytes 2752512 | tf_op args[0]
  2.7 0.1 broadcast_in_dim.8.mask
  2.8 1.8 %prologue.1 = (bf16[4,192,768]{2,1,0:T(8,128)(2,1)S(1)}, bf16[4,192,768]{2,1,0:T(8,128)(2,1)S(1)}, bf16[192,128]{1,0:T(8,128)(2,1)S(1)}, f32[128,128]{1,0:T(8,128)}) custom-call(bf16[2,24,28,512]{3,2,1,0:T(8,128)(2,1)S(1)} %copy.8.density, f32[192,128]{1,0:T(8,128)S(1)} %broadcast_in_dim.8.mask, bf16[512,128]{1,0:T(8,128)(2,1)S(1)} %copy-done.2, ...), custom_call_target="tpu_custom_call" | custom-call | tf_op jit(solution)/shard_map/prologue/pallas_call | solution.py:73
  4.6 2.7 %collective-permute-start = (bf16[4,192,768]{2,1,0:T(8,128)(2,1)S(1)}, bf16[4,192,768]{2,1,0:T(8,128)(2,1)}, u32[]{:S(2)}, u32[]{:S(2)}) collective-permute-start(bf16[4,192,768]{2,1,0:T(8,128)(2,1)S(1)} %get-tuple-element.15.high), channel_id=1, source_target_pairs={{0,1},{1,2},{2,3},{3,4},{4,5},{5,6},{6,7},{7,8},{8,9},{9,10},{10,1... | collective-permute-start | bytes 3538952 | tf_op jit(solution)/shard_map/ppermute | solution.py:498
  7.3 0.0 collective-permute-start.1
  7.3 18.0 %near_inner.1 = (f32[2,2,2,192,512]{4,3,2,1,0:T(8,128)}, bf16[16,512,512]{2,1,0:T(8,128)(2,1)}) custom-call(bf16[4,192,768]{2,1,0:T(8,128)(2,1)} %copy-done.3, bf16[4,192,768]{2,1,0:T(8,128)(2,1)} %copy-done.4, bf16[14,512,512]{2,1,0:T(8,128)(2,1)} %tables_in.2), custom_call_target="tpu_custom_call" | custom-call | flops 10000000000 | bytes 20000000 | tf_op jit(solution)/shard_map/near_inner/pallas_call | solution.py:235
  25.3 8.9 %collective-permute-start.4 = (bf16[192,128]{1,0:T(8,128)(2,1)S(1)}, bf16[192,128]{1,0:T(8,128)(2,1)S(1)}, u32[]{:S(2)}, u32[]{:S(2)}) collective-permute-start(bf16[192,128]{1,0:T(8,128)(2,1)S(1)} %get-tuple-element.19.own), channel_id=1, source_target_pairs={{0,3},{2,5},{4,7},{6,9},{8,11},{10,13},{12,15},{14,17},{16,19},{18... | collective-permute-start | bytes 147464 | tf_op jit(solution)/shard_map/ppermute | solution.py:511
  34.2 0.5 collective-permute-start.3
  34.7 1.0 %collective-permute-start.2 = (bf16[192,128]{1,0:T(8,128)(2,1)S(1)}, bf16[192,128]{1,0:T(8,128)(2,1)S(1)}, u32[]{:S(2)}, u32[]{:S(2)}) collective-permute-start(bf16[192,128]{1,0:T(8,128)(2,1)S(1)} %get-tuple-element.19.own), channel_id=1, source_target_pairs={{0,2},{1,3},{2,4},{3,5},{4,6},{5,7},{6,8},{7,9},{8,10},{9,11},{10,... | collective-permute-start | bytes 147464 | tf_op jit(solution)/shard_map/ppermute | solution.py:508
  35.7 7.3 %all-to-all-start = ((f32[128,1,128]{2,1,0:T(1,128)}), f32[128,1,128]{2,1,0:T(1,128)S(1)}, u32[]{:S(2)}, u32[]{:S(2)}) async-start(f32[128,1,128]{2,1,0:T(1,128)} %bitcast.8), calls=%async_computation | async-start | bytes 131072 | tf_op jit(solution)/shard_map/all_to_all | solution.py:507
  43.1 0.1 stack.23
  43.2 0.5 convert_element_type.11.kept
  43.7 0.0 collective-permute-done.below
  43.7 0.0 collective-permute-done.1.above
  43.7 12.5 %near_outer.1.near_in = f32[2,2,2,192,512]{4,3,2,1,0:T(8,128)} custom-call(f32[5]{0:T(128)} %convert_element_type.11.kept, bf16[4,192,768]{2,1,0:T(8,128)(2,1)} %copy-done.3, bf16[4,192,768]{2,1,0:T(8,128)(2,1)} %copy-done.4, bf16[4,192,768]{2,1,0:T(8,128)(2,1)} %collective-permute-done.below, bf16[4,192,768]{2,1,0:T(8,128)(2,1)} %collective-permute-done.1.above, ...), custom_call_target="tpu_custom_call" | custom-call | flops 7000000000 | bytes 20000000 | tf_op jit(solution)/shard_map/near_outer/pallas_call | solution.py:276
  56.3 0.0 collective-permute-done.4.far3
  56.3 0.0 collective-permute-done.2.back2
  56.4 0.5 copy-done.7
  56.9 0.0 copy-done.8
  56.9 0.0 copy-done.9
  56.9 0.0 copy-done.6
  57.0 24.9 %transfer.1 = bf16[2,28,24,512]{3,2,1,0:T(8,128)(2,1)} custom-call(s32[1]{0:T(128)} %bitcast.parity, f32[5]{0:T(128)} %convert_element_type.11.kept, bf16[4,192,768]{2,1,0:T(8,128)(2,1)} %copy-done.3, bf16[4,192,768]{2,1,0:T(8,128)(2,1)} %collective-permute-done.below, bf16[4,192,768]{2,1,0:T(8,128)(2,1)} %collective-permute-done.1.above, ...), custom_call_target="tpu_custom_call" | custom-call | flops 12000000000 | bytes 20000000 | tf_op jit(solution)/shard_map/transfer/pallas_call | solution.py:464
  (20 shorter events, 0.0 us)
Async XLA Ops:
  0.0 2.8 %copy-start.2 = (bf16[512,128]{1,0:T(8,128)(2,1)S(1)}, bf16[512,128]{1,0:T(8,128)(2,1)}, u32[]{:S(2)}) copy-start(bf16[512,128]{1,0:T(8,128)(2,1)} %anterpolate.3) | copy-start | bytes 393220
  0.0 2.8 %copy-start.1 = (bf16[8,128,128]{2,1,0:T(8,128)(2,1)S(1)}, bf16[8,128,128]{2,1,0:T(8,128)(2,1)}, u32[]{:S(2)}) copy-start(bf16[8,128,128]{2,1,0:T(8,128)(2,1)} %param.9) | copy-start | bytes 786436
  2.8 22.5 %copy-start = (f32[192,128]{1,0:T(8,128)}, f32[192,128]{1,0:T(8,128)S(1)}, u32[]{:S(2)}) copy-start(f32[192,128]{1,0:T(8,128)S(1)} %broadcast_in_dim.8.mask) | copy-start | bytes 294916
  4.6 2.7 %copy-start.3 = (bf16[4,192,768]{2,1,0:T(8,128)(2,1)}, bf16[4,192,768]{2,1,0:T(8,128)(2,1)S(1)}, u32[]{:S(2)}) copy-start(bf16[4,192,768]{2,1,0:T(8,128)(2,1)S(1)} %get-tuple-element.14.low) | copy-start | bytes 3538948
  4.6 2.7 %copy-start.4 = (bf16[4,192,768]{2,1,0:T(8,128)(2,1)}, bf16[4,192,768]{2,1,0:T(8,128)(2,1)S(1)}, u32[]{:S(2)}) copy-start(bf16[4,192,768]{2,1,0:T(8,128)(2,1)S(1)} %get-tuple-element.15.high) | copy-start | bytes 3538948
  4.6 30.1 %copy-start.5 = (bf16[192,128]{1,0:T(8,128)(2,1)}, bf16[192,128]{1,0:T(8,128)(2,1)S(1)}, u32[]{:S(2)}) copy-start(bf16[192,128]{1,0:T(8,128)(2,1)S(1)} %get-tuple-element.19.own) | copy-start | bytes 147460
  4.6 39.1 %collective-permute-start = (bf16[4,192,768]{2,1,0:T(8,128)(2,1)S(1)}, bf16[4,192,768]{2,1,0:T(8,128)(2,1)}, u32[]{:S(2)}, u32[]{:S(2)}) collective-permute-start(bf16[4,192,768]{2,1,0:T(8,128)(2,1)S(1)} %get-tuple-element.15.high), channel_id=1, source_target_pairs={{0,1},{1,2},{2,3},{3,4},{4,5},{5,6},{6,7},{7,8},{8,9},{9,10},{10,1... | collective-permute-start | bytes 3538952 | tf_op jit(solution)/shard_map/ppermute | solution.py:498
  7.3 36.5 %collective-permute-start.1 = (bf16[4,192,768]{2,1,0:T(8,128)(2,1)S(1)}, bf16[4,192,768]{2,1,0:T(8,128)(2,1)}, u32[]{:S(2)}, u32[]{:S(2)}) collective-permute-start(bf16[4,192,768]{2,1,0:T(8,128)(2,1)S(1)} %get-tuple-element.14.low), channel_id=1, source_target_pairs={{0,127},{1,0},{2,1},{3,2},{4,3},{5,4},{6,5},{7,6},{8,7},{9,8},{10,... | collective-permute-start | bytes 3538952 | tf_op jit(solution)/shard_map/ppermute | solution.py:499
  25.3 31.0 %collective-permute-start.4 = (bf16[192,128]{1,0:T(8,128)(2,1)S(1)}, bf16[192,128]{1,0:T(8,128)(2,1)S(1)}, u32[]{:S(2)}, u32[]{:S(2)}) collective-permute-start(bf16[192,128]{1,0:T(8,128)(2,1)S(1)} %get-tuple-element.19.own), channel_id=1, source_target_pairs={{0,3},{2,5},{4,7},{6,9},{8,11},{10,13},{12,15},{14,17},{16,19},{18... | collective-permute-start | bytes 147464 | tf_op jit(solution)/shard_map/ppermute | solution.py:511
  34.2 22.1 %collective-permute-start.3 = (bf16[192,128]{1,0:T(8,128)(2,1)S(1)}, bf16[192,128]{1,0:T(8,128)(2,1)S(1)}, u32[]{:S(2)}, u32[]{:S(2)}) collective-permute-start(bf16[192,128]{1,0:T(8,128)(2,1)S(1)} %get-tuple-element.19.own), channel_id=1, source_target_pairs={{0,126},{1,127},{2,0},{3,1},{4,2},{5,3},{6,4},{7,5},{8,6},{9,7},{1... | collective-permute-start | bytes 147464 | tf_op jit(solution)/shard_map/ppermute | solution.py:509
  34.7 21.6 %collective-permute-start.2 = (bf16[192,128]{1,0:T(8,128)(2,1)S(1)}, bf16[192,128]{1,0:T(8,128)(2,1)S(1)}, u32[]{:S(2)}, u32[]{:S(2)}) collective-permute-start(bf16[192,128]{1,0:T(8,128)(2,1)S(1)} %get-tuple-element.19.own), channel_id=1, source_target_pairs={{0,2},{1,3},{2,4},{3,5},{4,6},{5,7},{6,8},{7,9},{8,10},{9,11},{10,... | collective-permute-start | bytes 147464 | tf_op jit(solution)/shard_map/ppermute | solution.py:508
  35.7 20.6 %all-to-all-start = ((f32[128,1,128]{2,1,0:T(1,128)}), f32[128,1,128]{2,1,0:T(1,128)S(1)}, u32[]{:S(2)}, u32[]{:S(2)}) async-start(f32[128,1,128]{2,1,0:T(1,128)} %bitcast.8), calls=%async_computation | async-start | bytes 131072 | tf_op jit(solution)/shard_map/all_to_all | solution.py:507
  56.3 0.6 copy-start.7
  56.3 0.6 copy-start.8
  56.3 0.6 copy-start.9
  56.3 0.6 copy-start.6

commit v3 on v2

--- a/solution.py
+++ b/solution.py
@@ -397,22 +397,26 @@
     coarse_lines(far3[...].astype(F32) * kept[4], stage, 5 - 5 * side, lines)
 
     operators.wait()
-    for pz in range(2):
-
-        @pl.when(side == pz)
-        def _():
-            for py in range(2):
-                total = None
-                for jz in range(-2, 4):
-                    for term in transfer_terms(
-                        tables,
-                        jz - pz,
-                        range(-2, 4),
-                        py,
-                        lambda jy, jx: lines[jz + 2, jy + 2, :, (jx + 2) * K : (jx + 3) * K],
-                    ):
-                        total = term if total is None else total + term
-                coarse[py] = 0.5 * total
+    coarse[...] = jnp.zeros_like(coarse)
+    fine[...] = jnp.zeros_like(fine)
+    for py in range(2):
+        for dz in range(-3, 4):
+            layers = [pz for pz in range(2) if -2 <= dz + pz <= 3]
+            slot = jnp.clip(dz + side + 2, 0, 5)
+
+            def source(jy, jx):
+                lines_here = pl.ds(GROUP * (1 + jy // 2), ROWS)
+                lanes = slice((jx + 2) * K, (jx + 3) * K)
+                here = [leaves[dz + pz + 2, jy % 2, lines_here, lanes] for pz in layers]
+                return jnp.concatenate(here + [lines[slot, jy + 2, :, lanes]], axis=0)
+
+            for term in transfer_terms(tables, dz, range(-2, 4), py, source):
+                for n, pz in enumerate(layers):
+                    fine[pz * 2 + py] += term[n * ROWS : n * ROWS + ROWS]
+                wider = term[len(layers) * ROWS :]
+                if abs(dz) == 3:
+                    wider = jnp.where(side == (dz < 0), wider, 0.0)
+                coarse[py] += 0.5 * wider
 
     for py in range(2):
         for px in range(2):
@@ -426,26 +430,11 @@
     leaf_count = 2.0 * 24 * 28 * 128
     factor = wide(mask[...] * (leaf_count * PTS / total_charge))
 
-    for py in range(2):
-        for pz in range(2):
-            first = (4 * pz + 2 * py) * K
-            fine[pz * 2 + py] = mul_t(parent_local, merge[first : first + 2 * K, :])
-        for dz in range(-3, 4):
-            layers = [pz for pz in range(2) if -2 <= dz + pz <= 3]
-
-            def source(jy, jx):
-                lines_here = pl.ds(GROUP * (1 + jy // 2), ROWS)
-                here = [leaves[dz + pz + 2, jy % 2, lines_here, (jx + 2) * K : (jx + 3) * K] for pz in layers]
-                return jnp.concatenate(here, axis=0)
-
-            for term in transfer_terms(tables, dz, range(-2, 4), py, source):
-                for n, pz in enumerate(layers):
-                    fine[pz * 2 + py] += term[n * ROWS : n * ROWS + ROWS]
-
     near_part.wait()
     for pz in range(2):
         for py in range(2):
-            total = fine[pz * 2 + py]
+            first = (4 * pz + 2 * py) * K
+            total = fine[pz * 2 + py] + mul_t(parent_local, merge[first : first + 2 * K, :])
             local = total.astype(BF16)
             for px in range(2):
                 far = mul_t(local[:, px * K : px * K + K], anterpolate[...])
@@ -497,14 +486,14 @@
     place = lax.axis_index("leaf")
     below = lax.ppermute(high, "leaf", around(count, 1))
     above = lax.ppermute(low, "leaf", around(count, -1))
+    charge = lax.all_to_all(partial, "leaf", 0, 0, tiled=True)
     parity = place % 2
     source3 = place + 3 - 6 * parity
     kept = jnp.stack(
         [place >= 1, place < count - 1, place >= 2, place < count - 2, (source3 >= 0) & (source3 < count)]
     ).astype(F32)
     near, outer = near_inner(low, high, near_tables)
-    partial, own, near = lax.optimization_barrier((partial, own, near))
-    charge = lax.all_to_all(partial, "leaf", 0, 0, tiled=True)
+    own, near = lax.optimization_barrier((own, near))
     back2 = lax.ppermute(own, "leaf", around(count, 2))
     ahead2 = lax.ppermute(own, "leaf", around(count, -2))
     crossed = [(i, (i + 3) % count) for i in range(0, count, 2)]

time: 82.2 us -> 77.3 us (0.940)
  Pallas kernels: 57.2 us -> 52.2 us
    pallas_call x1, Pallas kernels: 24.9 us -> 19.9 us  [transfer(): pl.pallas_call(transfer_kernel, name='transfer', out_shape=jax.ShapeDtype...]
  transfers between devices with their start and end apart: 6 -> 6, of which waited for: 0 -> 0; matrix products, arithmetic and copies ran while one was open for 1% -> 1% of each run, Pallas kernels for 37% -> 40%
where the time goes in v3:
time: 77.3 us; the launch traced here: 77.1 us
  Pallas kernels  52.2 us (68%)
  starting transfers between devices  20.4 us (26%)
  local copies, waits for them, and re-layouts  2.75 us (4%)
  other arithmetic  1.29 us (2%)
    pallas_call x1, Pallas kernels, transfer(): pl.pallas_call(transfer_kernel, name='transfer', out_shape=jax.ShapeDtype...  19.9 us
    pallas_call x1, Pallas kernels, near_inner(): pl.pallas_call(near_inner_kernel, name='near_inner', out_shape=(jax.Shape...  18 us
    pallas_call x1, Pallas kernels, near_outer(): pl.pallas_call(near_outer_kernel, name='near_outer', out_shape=jax.ShapeD...  12.5 us
    ppermute x1, starting transfers between devices, body(): far3 = lax.ppermute(own, 'leaf', crossed + [(j, i) for i, j in crossed])  8.92 us
    all_to_all x1, starting transfers between devices, body(): charge = lax.all_to_all(partial, 'leaf', 0, 0, tiled=True)  7.33 us
    ppermute x1, starting transfers between devices, body(): below = lax.ppermute(high, 'leaf', around(count, 1))  2.69 us
    unnamed x22, local copies, waits for them, and re-layouts  2.48 us
    pallas_call x1, Pallas kernels, prologue(): pl.pallas_call(prologue_kernel, name='prologue', out_shape=(pack, pack, j...  1.79 us
  transfers between devices with their start and end apart: 6, of which 0 were waited for; matrix products, arithmetic and copies ran while one was open for 1% of the time, Pallas kernels for 40%

profile of v3, /device:TPU:1, one launch (start us, length us, event | category | flops | bytes accessed | tf_op | source)
XLA Modules:
  0.0 77.1 jit_solution(5819978992338099479)
XLA Ops:
  0.0 0.7 convert_element_type.12
  0.8 0.1 broadcast_in_dim.7
  0.8 1.8 %copy.8.density = bf16[2,24,28,512]{3,2,1,0:T(8,128)(2,1)S(1)} copy(bf16[2,24,28,512]{3,1,2,0:T(8,128)(2,1)} %param.6) | data formatting | bytes 2752512 | tf_op args[0]
  2.7 0.1 broadcast_in_dim.8.mask
  2.8 1.8 %prologue.1 = (bf16[4,192,768]{2,1,0:T(8,128)(2,1)S(1)}, bf16[4,192,768]{2,1,0:T(8,128)(2,1)S(1)}, bf16[192,128]{1,0:T(8,128)(2,1)S(1)}, f32[128,128]{1,0:T(8,128)}) custom-call(bf16[2,24,28,512]{3,2,1,0:T(8,128)(2,1)S(1)} %copy.8.density, f32[192,128]{1,0:T(8,128)S(1)} %broadcast_in_dim.8.mask, bf16[512,128]{1,0:T(8,128)(2,1)S(1)} %copy-done.2, ...), custom_call_target="tpu_custom_call" | custom-call | tf_op jit(solution)/shard_map/prologue/pallas_call | solution.py:73
  4.6 2.7 %collective-permute-start = (bf16[4,192,768]{2,1,0:T(8,128)(2,1)S(1)}, bf16[4,192,768]{2,1,0:T(8,128)(2,1)}, u32[]{:S(2)}, u32[]{:S(2)}) collective-permute-start(bf16[4,192,768]{2,1,0:T(8,128)(2,1)S(1)} %get-tuple-element.14.high), channel_id=1, source_target_pairs={{0,1},{1,2},{2,3},{3,4},{4,5},{5,6},{6,7},{7,8},{8,9},{9,10},{10,1... | collective-permute-start | bytes 3538952 | tf_op jit(solution)/shard_map/ppermute | solution.py:487
  7.3 0.0 collective-permute-start.1
  7.3 18.0 %near_inner.1 = (f32[2,2,2,192,512]{4,3,2,1,0:T(8,128)}, bf16[16,512,512]{2,1,0:T(8,128)(2,1)}) custom-call(bf16[4,192,768]{2,1,0:T(8,128)(2,1)} %copy-done.3, bf16[4,192,768]{2,1,0:T(8,128)(2,1)} %copy-done.4, bf16[14,512,512]{2,1,0:T(8,128)(2,1)} %tables_in.2), custom_call_target="tpu_custom_call" | custom-call | flops 10000000000 | bytes 20000000 | tf_op jit(solution)/shard_map/near_inner/pallas_call | solution.py:235
  25.3 8.9 %collective-permute-start.4 = (bf16[192,128]{1,0:T(8,128)(2,1)S(1)}, bf16[192,128]{1,0:T(8,128)(2,1)S(1)}, u32[]{:S(2)}, u32[]{:S(2)}) collective-permute-start(bf16[192,128]{1,0:T(8,128)(2,1)S(1)} %get-tuple-element.17.own), channel_id=1, source_target_pairs={{0,3},{2,5},{4,7},{6,9},{8,11},{10,13},{12,15},{14,17},{16,19},{18... | collective-permute-start | bytes 147464 | tf_op jit(solution)/shard_map/ppermute | solution.py:500
  34.2 0.5 collective-permute-start.3
  34.7 1.0 %collective-permute-start.2 = (bf16[192,128]{1,0:T(8,128)(2,1)S(1)}, bf16[192,128]{1,0:T(8,128)(2,1)S(1)}, u32[]{:S(2)}, u32[]{:S(2)}) collective-permute-start(bf16[192,128]{1,0:T(8,128)(2,1)S(1)} %get-tuple-element.17.own), channel_id=1, source_target_pairs={{0,2},{1,3},{2,4},{3,5},{4,6},{5,7},{6,8},{7,9},{8,10},{9,11},{10,... | collective-permute-start | bytes 147464 | tf_op jit(solution)/shard_map/ppermute | solution.py:497
  35.7 7.3 %all-to-all-start = ((f32[128,1,128]{2,1,0:T(1,128)}), f32[128,1,128]{2,1,0:T(1,128)S(1)}, u32[]{:S(2)}, u32[]{:S(2)}) async-start(f32[128,1,128]{2,1,0:T(1,128)} %bitcast.8), calls=%async_computation | async-start | bytes 131072 | tf_op jit(solution)/shard_map/all_to_all | solution.py:489
  43.1 0.1 stack.23
  43.2 0.5 convert_element_type.11.kept
  43.7 0.0 collective-permute-done.below
  43.7 0.0 collective-permute-done.1.above
  43.7 12.5 %near_outer.1.near_in = f32[2,2,2,192,512]{4,3,2,1,0:T(8,128)} custom-call(f32[5]{0:T(128)} %convert_element_type.11.kept, bf16[4,192,768]{2,1,0:T(8,128)(2,1)} %copy-done.3, bf16[4,192,768]{2,1,0:T(8,128)(2,1)} %copy-done.4, bf16[4,192,768]{2,1,0:T(8,128)(2,1)} %collective-permute-done.below, bf16[4,192,768]{2,1,0:T(8,128)(2,1)} %collective-permute-done.1.above, ...), custom_call_target="tpu_custom_call" | custom-call | flops 7000000000 | bytes 20000000 | tf_op jit(solution)/shard_map/near_outer/pallas_call | solution.py:276
  56.3 0.0 collective-permute-done.4.far3
  56.3 0.0 collective-permute-done.3.ahead2
  56.4 0.5 copy-done.7
  56.9 0.0 copy-done.8
  56.9 0.0 copy-done.9
  56.9 0.0 copy-done.6
  57.0 19.9 %transfer.1 = bf16[2,28,24,512]{3,2,1,0:T(8,128)(2,1)} custom-call(s32[1]{0:T(128)} %bitcast.parity, f32[5]{0:T(128)} %convert_element_type.11.kept, bf16[4,192,768]{2,1,0:T(8,128)(2,1)} %copy-done.3, bf16[4,192,768]{2,1,0:T(8,128)(2,1)} %collective-permute-done.below, bf16[4,192,768]{2,1,0:T(8,128)(2,1)} %collective-permute-done.1.above, ...), custom_call_target="tpu_custom_call" | custom-call | flops 12000000000 | bytes 20000000 | tf_op jit(solution)/shard_map/transfer/pallas_call | solution.py:453
  (20 shorter events, 0.0 us)
Async XLA Ops:
  0.0 2.8 %copy-start.2 = (bf16[512,128]{1,0:T(8,128)(2,1)S(1)}, bf16[512,128]{1,0:T(8,128)(2,1)}, u32[]{:S(2)}) copy-start(bf16[512,128]{1,0:T(8,128)(2,1)} %anterpolate.3) | copy-start | bytes 393220
  0.0 2.8 %copy-start.1 = (bf16[8,128,128]{2,1,0:T(8,128)(2,1)S(1)}, bf16[8,128,128]{2,1,0:T(8,128)(2,1)}, u32[]{:S(2)}) copy-start(bf16[8,128,128]{2,1,0:T(8,128)(2,1)} %param.9) | copy-start | bytes 786436
  2.8 22.5 %copy-start = (f32[192,128]{1,0:T(8,128)}, f32[192,128]{1,0:T(8,128)S(1)}, u32[]{:S(2)}) copy-start(f32[192,128]{1,0:T(8,128)S(1)} %broadcast_in_dim.8.mask) | copy-start | bytes 294916
  4.6 2.7 %copy-start.3 = (bf16[4,192,768]{2,1,0:T(8,128)(2,1)}, bf16[4,192,768]{2,1,0:T(8,128)(2,1)S(1)}, u32[]{:S(2)}) copy-start(bf16[4,192,768]{2,1,0:T(8,128)(2,1)S(1)} %get-tuple-element.13.low) | copy-start | bytes 3538948
  4.6 2.7 %copy-start.4 = (bf16[4,192,768]{2,1,0:T(8,128)(2,1)}, bf16[4,192,768]{2,1,0:T(8,128)(2,1)S(1)}, u32[]{:S(2)}) copy-start(bf16[4,192,768]{2,1,0:T(8,128)(2,1)S(1)} %get-tuple-element.14.high) | copy-start | bytes 3538948
  4.6 30.1 %copy-start.5 = (bf16[192,128]{1,0:T(8,128)(2,1)}, bf16[192,128]{1,0:T(8,128)(2,1)S(1)}, u32[]{:S(2)}) copy-start(bf16[192,128]{1,0:T(8,128)(2,1)S(1)} %get-tuple-element.17.own) | copy-start | bytes 147460
  4.6 39.1 %collective-permute-start = (bf16[4,192,768]{2,1,0:T(8,128)(2,1)S(1)}, bf16[4,192,768]{2,1,0:T(8,128)(2,1)}, u32[]{:S(2)}, u32[]{:S(2)}) collective-permute-start(bf16[4,192,768]{2,1,0:T(8,128)(2,1)S(1)} %get-tuple-element.14.high), channel_id=1, source_target_pairs={{0,1},{1,2},{2,3},{3,4},{4,5},{5,6},{6,7},{7,8},{8,9},{9,10},{10,1... | collective-permute-start | bytes 3538952 | tf_op jit(solution)/shard_map/ppermute | solution.py:487
  7.3 36.4 %collective-permute-start.1 = (bf16[4,192,768]{2,1,0:T(8,128)(2,1)S(1)}, bf16[4,192,768]{2,1,0:T(8,128)(2,1)}, u32[]{:S(2)}, u32[]{:S(2)}) collective-permute-start(bf16[4,192,768]{2,1,0:T(8,128)(2,1)S(1)} %get-tuple-element.13.low), channel_id=1, source_target_pairs={{0,127},{1,0},{2,1},{3,2},{4,3},{5,4},{6,5},{7,6},{8,7},{9,8},{10,... | collective-permute-start | bytes 3538952 | tf_op jit(solution)/shard_map/ppermute | solution.py:488
  25.3 31.0 %collective-permute-start.4 = (bf16[192,128]{1,0:T(8,128)(2,1)S(1)}, bf16[192,128]{1,0:T(8,128)(2,1)S(1)}, u32[]{:S(2)}, u32[]{:S(2)}) collective-permute-start(bf16[192,128]{1,0:T(8,128)(2,1)S(1)} %get-tuple-element.17.own), channel_id=1, source_target_pairs={{0,3},{2,5},{4,7},{6,9},{8,11},{10,13},{12,15},{14,17},{16,19},{18... | collective-permute-start | bytes 147464 | tf_op jit(solution)/shard_map/ppermute | solution.py:500
  34.2 22.1 %collective-permute-start.3 = (bf16[192,128]{1,0:T(8,128)(2,1)S(1)}, bf16[192,128]{1,0:T(8,128)(2,1)S(1)}, u32[]{:S(2)}, u32[]{:S(2)}) collective-permute-start(bf16[192,128]{1,0:T(8,128)(2,1)S(1)} %get-tuple-element.17.own), channel_id=1, source_target_pairs={{0,126},{1,127},{2,0},{3,1},{4,2},{5,3},{6,4},{7,5},{8,6},{9,7},{1... | collective-permute-start | bytes 147464 | tf_op jit(solution)/shard_map/ppermute | solution.py:498
  34.7 21.6 %collective-permute-start.2 = (bf16[192,128]{1,0:T(8,128)(2,1)S(1)}, bf16[192,128]{1,0:T(8,128)(2,1)S(1)}, u32[]{:S(2)}, u32[]{:S(2)}) collective-permute-start(bf16[192,128]{1,0:T(8,128)(2,1)S(1)} %get-tuple-element.17.own), channel_id=1, source_target_pairs={{0,2},{1,3},{2,4},{3,5},{4,6},{5,7},{6,8},{7,9},{8,10},{9,11},{10,... | collective-permute-start | bytes 147464 | tf_op jit(solution)/shard_map/ppermute | solution.py:497
  35.7 20.6 %all-to-all-start = ((f32[128,1,128]{2,1,0:T(1,128)}), f32[128,1,128]{2,1,0:T(1,128)S(1)}, u32[]{:S(2)}, u32[]{:S(2)}) async-start(f32[128,1,128]{2,1,0:T(1,128)} %bitcast.8), calls=%async_computation | async-start | bytes 131072 | tf_op jit(solution)/shard_map/all_to_all | solution.py:489
  56.3 0.6 copy-start.7
  56.3 0.6 copy-start.8
  56.3 0.6 copy-start.9
  56.3 0.6 copy-start.6

commit v4 on v3

--- a/solution.py
+++ b/solution.py
@@ -1,6 +1,7 @@
+import functools
+
 import jax
 import jax.numpy as jnp
-import numpy as np
 from jax import lax
 from jax.experimental import pallas as pl
 from jax.experimental.pallas import tpu as pltpu
@@ -53,7 +54,7 @@
                     packs[z][py * 2 + px, rows, 0:PTS] = part.astype(BF16)
         return total
 
-    total = lax.fori_loop(0, LINES, line, jnp.zeros((GROUP, PTS), F32))
+    total = lax.fori_loop(0, LINES, line, jnp.zeros((GROUP, PTS), F32), unroll=4)
     partial[...] = jnp.broadcast_to(jnp.sum(total), partial.shape)
     for z in range(2):
         found = mul(packs[z][:, :, 0:PTS].reshape(4 * ROWS, PTS), anterpolate[...]).astype(BF16)
@@ -108,7 +109,7 @@
                     outer[b * 4 + c, rows, lanes] = along_y[b].astype(BF16)
         return 0
 
-    lax.fori_loop(0, PTS // 16, chunk, 0)
+    lax.fori_loop(0, PTS // 16, chunk, 0, unroll=4)
 
 
 def inner_weights(tables, outer, inner):
@@ -133,7 +134,7 @@
             inner[10 + k, here, there] = (0.5 * (ends - flat)).astype(BF16)
         return 0
 
-    lax.fori_loop(0, 16, block, 0)
+    lax.fori_loop(0, 16, block, 0, unroll=4)
 
 
 def spread_line(load, store):
@@ -176,14 +177,14 @@
             spread_line(load, store)
         return 0
 
-    lax.fori_loop(0, LINES, line, 0)
+    lax.fori_loop(0, LINES, line, 0, unroll=4)
 
 
 def gathered_products(product, held, made):
     for b in range(4):
         for c in range(4):
-            made[c] = product(b, c)
-        p = [made[c] for c in range(4)]
+            made[4 * b + c] = product(b, c)
+        p = [made[4 * b + c] for c in range(4)]
         sides = (p[0] + p[1] + p[2], p[1] - p[2] - p[3])
         for px in range(2):
             value = sides[px]
@@ -222,12 +223,10 @@
 
         return one
 
-    gathered_products(product(0), held, made)
-    near[0] = held[...]
-    near[1] = held[...]
-    gathered_products(product(1), held, made)
-    near[0] += held[...]
-    near[1] -= held[...]
+    for a in range(2):
+        gathered_products(product(a), held.at[a], made)
+    near[0] = held[0] + held[1]
+    near[1] = held[0] - held[1]
     leaving.wait()
 
 
@@ -244,8 +243,8 @@
         scratch_shapes=[
             pltpu.VMEM((32, ROWS, PTS), BF16),
             pltpu.VMEM((20, PTS, PTS), BF16),
-            pltpu.VMEM((2, 2, ROWS, PTS), F32),
-            pltpu.VMEM((4, ROWS, PTS), F32),
+            pltpu.VMEM((2, 2, 2, ROWS, PTS), F32),
+            pltpu.VMEM((16, ROWS, PTS), F32),
             pltpu.VMEM((14, PTS, PTS), BF16),
             pltpu.VMEM((16, PTS, PTS), BF16),
             pltpu.SemaphoreType.DMA((3,)),
@@ -255,7 +254,14 @@
     )(low, high, tables)
 
 
-def near_outer_kernel(kept, low, high, below, above, outer_in, near_in, near, parts, held, made, outer, sems):
+def flags(place, count):
+    third = place + 3 - 6 * (place % 2)
+    found = (place >= 1, place < count - 1, place >= 2, place < count - 2, (third >= 0) & (third < count))
+    return [jnp.where(f, 1.0, 0.0) for f in found]
+
+
+def near_outer_kernel(count, place, low, high, below, above, outer_in, near_in, near, parts, held, made, outer, sems):
+    kept = flags(place[0], count)
     weights = pltpu.make_async_copy(outer_in, outer, sems.at[0])
     inner_part = pltpu.make_async_copy(near_in, near, sems.at[1])
     weights.start()
@@ -272,9 +278,9 @@
     near[1] -= held[...]
 
 
-def near_outer(kept, low, high, below, above, outer, near):
+def near_outer(count, place, low, high, below, above, outer, near):
     return pl.pallas_call(
-        near_outer_kernel,
+        functools.partial(near_outer_kernel, count),
         name="near_outer",
         out_shape=jax.ShapeDtypeStruct((2, 2, 2, ROWS, PTS), F32),
         in_specs=[SMEM] + [VMEM] * 4 + [ANY] * 2,
@@ -282,13 +288,13 @@
         scratch_shapes=[
             pltpu.VMEM((32, ROWS, PTS), BF16),
             pltpu.VMEM((2, 2, ROWS, PTS), F32),
-            pltpu.VMEM((4, ROWS, PTS), F32),
+            pltpu.VMEM((16, ROWS, PTS), F32),
             pltpu.VMEM((16, PTS, PTS), BF16),
             pltpu.SemaphoreType.DMA((2,)),
         ],
         cost_estimate=pl.CostEstimate(flops=7_000_000_000, bytes_accessed=20_000_000, transcendentals=0),
         compiler_params=pltpu.CompilerParams(vmem_limit_bytes=60 << 20),
-    )(kept, low, high, below, above, outer, near)
+    )(place, low, high, below, above, outer, near)
 
 
 def positive_offsets(radius, minimum):
@@ -372,9 +378,10 @@
 
 
 def transfer_kernel(
-    parity, kept, low, below, above, own, back2, ahead2, far3, mask, charge, merge, anterpolate, tables_in, near_in,
+    count, place, low, below, above, own, back2, ahead2, far3, mask, charge, merge, anterpolate, tables_in, near_in,
     potential, leaves, lines, stage, weave, flat, coarse, tables, near, fine, sems,
 ):
+    kept = flags(place[0], count)
     operators = pltpu.make_async_copy(tables_in, tables, sems.at[0])
     near_part = pltpu.make_async_copy(near_in, near, sems.at[1])
     operators.start()
@@ -389,7 +396,7 @@
             if n < 2 or n > 3:
                 even, odd = even * kept[n // 4], odd * kept[n // 4]
             leaves[n, py, GROUP : GROUP + ROWS, :] = neighbours(even, odd, ROWS)
-    side = parity[0]
+    side = place[0] % 2
     boxes = (back2[...], merged(below, merge), own[...], merged(above, merge), ahead2[...])
     for n, (box, flag) in enumerate(zip(boxes, (2, 0, None, 1, 3))):
         box = box.astype(F32)
@@ -449,12 +456,12 @@
                 potential[pz, x, :, h * 128 : h * 128 + 128] = weave[h, x].astype(BF16)
 
 
-def transfer(parity, kept, low, below, above, own, back2, ahead2, far3, mask, charge, merge, anterpolate, tables, near):
+def transfer(count, place, low, below, above, own, back2, ahead2, far3, mask, charge, merge, anterpolate, tables, near):
     return pl.pallas_call(
-        transfer_kernel,
+        functools.partial(transfer_kernel, count),
         name="transfer",
         out_shape=jax.ShapeDtypeStruct((2, 28, 2 * LINES, PTS), BF16),
-        in_specs=[SMEM] * 2 + [VMEM] * 11 + [ANY] * 2,
+        in_specs=[SMEM] + [VMEM] * 11 + [ANY] * 2,
         out_specs=VMEM,
         scratch_shapes=[
             pltpu.VMEM((6, 2, ROWS + 2 * GROUP, 6 * K), BF16),
@@ -470,7 +477,7 @@
         ],
         cost_estimate=pl.CostEstimate(flops=12_000_000_000, bytes_accessed=20_000_000, transcendentals=0),
         compiler_params=pltpu.CompilerParams(vmem_limit_bytes=60 << 20),
-    )(parity, kept, low, below, above, own, back2, ahead2, far3, mask, charge, merge, anterpolate, tables, near)
+    )(place, low, below, above, own, back2, ahead2, far3, mask, charge, merge, anterpolate, tables, near)
 
 
 def around(count, step):
@@ -483,24 +490,19 @@
     mask = jnp.broadcast_to(present.reshape(ROWS, 1), (ROWS, 128))
     merge = merge_tables.reshape(8 * K, K)
     low, high, own, partial = prologue(density, mask, anterpolate, merge)
-    place = lax.axis_index("leaf")
+    place = lax.axis_index("leaf").reshape(1)
     below = lax.ppermute(high, "leaf", around(count, 1))
     above = lax.ppermute(low, "leaf", around(count, -1))
     charge = lax.all_to_all(partial, "leaf", 0, 0, tiled=True)
-    parity = place % 2
-    source3 = place + 3 - 6 * parity
-    kept = jnp.stack(
-        [place >= 1, place < count - 1, place >= 2, place < count - 2, (source3 >= 0) & (source3 < count)]
-    ).astype(F32)
     near, outer = near_inner(low, high, near_tables)
     own, near = lax.optimization_barrier((own, near))
     back2 = lax.ppermute(own, "leaf", around(count, 2))
     ahead2 = lax.ppermute(own, "leaf", around(count, -2))
     crossed = [(i, (i + 3) % count) for i in range(0, count, 2)]
     far3 = lax.ppermute(own, "leaf", crossed + [(j, i) for i, j in crossed])
-    near = near_outer(kept, low, high, below, above, outer, near)
+    near = near_outer(count, place, low, high, below, above, outer, near)
     potential = transfer(
-        parity.reshape(1), kept, low, below, above, own, back2, ahead2, far3, mask, charge, merge, anterpolate,
+        count, place, low, below, above, own, back2, ahead2, far3, mask, charge, merge, anterpolate,
         transfer_tables, near,
     )
     return jnp.swapaxes(potential, 1, 2)

time: 77.3 us -> 76 us (0.983)
  transfers between devices with their start and end apart: 6 -> 6, of which waited for: 0 -> 0; matrix products, arithmetic and copies ran while one was open for 1% -> 0% of each run, Pallas kernels for 40% -> 40%
where the time goes in v4:
time: 76 us; the launch traced here: 75.8 us
  Pallas kernels  51.6 us (68%)
  starting transfers between devices  20.4 us (27%)
  local copies, waits for them, and re-layouts  2.64 us (3%)
    pallas_call x1, Pallas kernels, transfer(): pl.pallas_call(functools.partial(transfer_kernel, count), name='transfer'...  19.9 us
    pallas_call x1, Pallas kernels, near_inner(): pl.pallas_call(near_inner_kernel, name='near_inner', out_shape=(jax.Shape...  17.4 us
    pallas_call x1, Pallas kernels, near_outer(): pl.pallas_call(functools.partial(near_outer_kernel, count), name='near_ou...  12.5 us
    ppermute x1, starting transfers between devices, body(): far3 = lax.ppermute(own, 'leaf', crossed + [(j, i) for i, j in crossed])  8.9 us
    all_to_all x1, starting transfers between devices, body(): charge = lax.all_to_all(partial, 'leaf', 0, 0, tiled=True)  7.33 us
    ppermute x1, starting transfers between devices, body(): below = lax.ppermute(high, 'leaf', around(count, 1))  2.69 us
    unnamed x22, local copies, waits for them, and re-layouts  2.47 us
    pallas_call x1, Pallas kernels, prologue(): pl.pallas_call(prologue_kernel, name='prologue', out_shape=(pack, pack, j...  1.76 us
  transfers between devices with their start and end apart: 6, of which 0 were waited for; matrix products, arithmetic and copies ran while one was open for 0% of the time, Pallas kernels for 40%

profile of v4, /device:TPU:1, one launch (start us, length us, event | category | flops | bytes accessed | tf_op | source)
XLA Modules:
  0.0 75.8 jit_solution(15796123681106834381)
XLA Ops:
  0.0 0.7 convert_element_type.8
  0.8 0.1 broadcast_in_dim.7
  0.8 1.8 %copy.8.density = bf16[2,24,28,512]{3,2,1,0:T(8,128)(2,1)S(1)} copy(bf16[2,24,28,512]{3,1,2,0:T(8,128)(2,1)} %param.6) | data formatting | bytes 2752512 | tf_op args[0]
  2.7 0.1 broadcast_in_dim.8.mask
  2.8 1.8 %prologue.1 = (bf16[4,192,768]{2,1,0:T(8,128)(2,1)S(1)}, bf16[4,192,768]{2,1,0:T(8,128)(2,1)S(1)}, bf16[192,128]{1,0:T(8,128)(2,1)S(1)}, f32[128,128]{1,0:T(8,128)}) custom-call(bf16[2,24,28,512]{3,2,1,0:T(8,128)(2,1)S(1)} %copy.8.density, f32[192,128]{1,0:T(8,128)S(1)} %broadcast_in_dim.8.mask, bf16[512,128]{1,0:T(8,128)(2,1)S(1)} %copy-done.2, ...), custom_call_target="tpu_custom_call" | custom-call | tf_op jit(solution)/shard_map/prologue/pallas_call | solution.py:74
  4.6 2.7 %collective-permute-start = (bf16[4,192,768]{2,1,0:T(8,128)(2,1)S(1)}, bf16[4,192,768]{2,1,0:T(8,128)(2,1)}, u32[]{:S(2)}, u32[]{:S(2)}) collective-permute-start(bf16[4,192,768]{2,1,0:T(8,128)(2,1)S(1)} %get-tuple-element.14.high), channel_id=1, source_target_pairs={{0,1},{1,2},{2,3},{3,4},{4,5},{5,6},{6,7},{7,8},{8,9},{9,10},{10,1... | collective-permute-start | bytes 3538952 | tf_op jit(solution)/shard_map/ppermute | solution.py:494
  7.2 0.0 collective-permute-start.1
  7.3 17.4 %near_inner.1 = (f32[2,2,2,192,512]{4,3,2,1,0:T(8,128)}, bf16[16,512,512]{2,1,0:T(8,128)(2,1)}) custom-call(bf16[4,192,768]{2,1,0:T(8,128)(2,1)} %copy-done.3, bf16[4,192,768]{2,1,0:T(8,128)(2,1)} %copy-done.4, bf16[14,512,512]{2,1,0:T(8,128)(2,1)} %tables_in.2), custom_call_target="tpu_custom_call" | custom-call | flops 10000000000 | bytes 20000000 | tf_op jit(solution)/shard_map/near_inner/pallas_call | solution.py:234
  24.7 8.9 %collective-permute-start.4 = (bf16[192,128]{1,0:T(8,128)(2,1)S(1)}, bf16[192,128]{1,0:T(8,128)(2,1)S(1)}, u32[]{:S(2)}, u32[]{:S(2)}) collective-permute-start(bf16[192,128]{1,0:T(8,128)(2,1)S(1)} %get-tuple-element.17.own), channel_id=1, source_target_pairs={{0,3},{2,5},{4,7},{6,9},{8,11},{10,13},{12,15},{14,17},{16,19},{18... | collective-permute-start | bytes 147464 | tf_op jit(solution)/shard_map/ppermute | solution.py:502
  33.6 0.5 collective-permute-start.3
  34.1 1.0 %collective-permute-start.2 = (bf16[192,128]{1,0:T(8,128)(2,1)S(1)}, bf16[192,128]{1,0:T(8,128)(2,1)S(1)}, u32[]{:S(2)}, u32[]{:S(2)}) collective-permute-start(bf16[192,128]{1,0:T(8,128)(2,1)S(1)} %get-tuple-element.17.own), channel_id=1, source_target_pairs={{0,2},{1,3},{2,4},{3,5},{4,6},{5,7},{6,8},{7,9},{8,10},{9,11},{10,... | collective-permute-start | bytes 147464 | tf_op jit(solution)/shard_map/ppermute | solution.py:499
  35.1 7.3 %all-to-all-start = ((f32[128,1,128]{2,1,0:T(1,128)}), f32[128,1,128]{2,1,0:T(1,128)S(1)}, u32[]{:S(2)}, u32[]{:S(2)}) async-start(f32[128,1,128]{2,1,0:T(1,128)} %bitcast.3), calls=%async_computation | async-start | bytes 131072 | tf_op jit(solution)/shard_map/all_to_all | solution.py:496
  42.4 0.0 collective-permute-done.below
  42.4 0.0 collective-permute-done.1.above
  42.5 12.5 %near_outer.1.near_in = f32[2,2,2,192,512]{4,3,2,1,0:T(8,128)} custom-call(s32[1]{0:T(128)} %bitcast.place, bf16[4,192,768]{2,1,0:T(8,128)(2,1)} %copy-done.3, bf16[4,192,768]{2,1,0:T(8,128)(2,1)} %copy-done.4, bf16[4,192,768]{2,1,0:T(8,128)(2,1)} %collective-permute-done.below, bf16[4,192,768]{2,1,0:T(8,128)(2,1)} %collective-permute-done.1.above, ...), custom_call_target="tpu_custom_call" | custom-call | flops 7000000000 | bytes 20000000 | tf_op jit(solution)/shard_map/near_outer/pallas_call | solution.py:282
  55.0 0.0 collective-permute-done.4.far3
  55.0 0.0 collective-permute-done.3.ahead2
  55.0 0.0 collective-permute-done.2.back2
  55.0 0.0 all-to-all-done
  55.1 0.5 copy-done.7
  55.6 0.0 copy-done.8
  55.6 0.0 copy-done.9
  55.6 0.0 copy-done.6
  55.7 19.9 %transfer.1 = bf16[2,28,24,512]{3,2,1,0:T(8,128)(2,1)} custom-call(s32[1]{0:T(128)} %bitcast.place, bf16[4,192,768]{2,1,0:T(8,128)(2,1)} %copy-done.3, bf16[4,192,768]{2,1,0:T(8,128)(2,1)} %collective-permute-done.below, bf16[4,192,768]{2,1,0:T(8,128)(2,1)} %collective-permute-done.1.above, bf16[192,128]{1,0:T(8,128)(2,1)} %copy-done.5, ...), custom_call_target="tpu_custom_call" | custom-call | flops 12000000000 | bytes 20000000 | tf_op jit(solution)/shard_map/transfer/pallas_call | solution.py:460
  (18 shorter events, 0.0 us)
Async XLA Ops:
  0.0 2.8 %copy-start.2 = (bf16[512,128]{1,0:T(8,128)(2,1)S(1)}, bf16[512,128]{1,0:T(8,128)(2,1)}, u32[]{:S(2)}) copy-start(bf16[512,128]{1,0:T(8,128)(2,1)} %anterpolate.3) | copy-start | bytes 393220
  0.0 2.8 %copy-start.1 = (bf16[8,128,128]{2,1,0:T(8,128)(2,1)S(1)}, bf16[8,128,128]{2,1,0:T(8,128)(2,1)}, u32[]{:S(2)}) copy-start(bf16[8,128,128]{2,1,0:T(8,128)(2,1)} %param.9) | copy-start | bytes 786436
  2.8 21.9 %copy-start = (f32[192,128]{1,0:T(8,128)}, f32[192,128]{1,0:T(8,128)S(1)}, u32[]{:S(2)}) copy-start(f32[192,128]{1,0:T(8,128)S(1)} %broadcast_in_dim.8.mask) | copy-start | bytes 294916
  4.6 2.7 %copy-start.3 = (bf16[4,192,768]{2,1,0:T(8,128)(2,1)}, bf16[4,192,768]{2,1,0:T(8,128)(2,1)S(1)}, u32[]{:S(2)}) copy-start(bf16[4,192,768]{2,1,0:T(8,128)(2,1)S(1)} %get-tuple-element.13.low) | copy-start | bytes 3538948
  4.6 2.7 %copy-start.4 = (bf16[4,192,768]{2,1,0:T(8,128)(2,1)}, bf16[4,192,768]{2,1,0:T(8,128)(2,1)S(1)}, u32[]{:S(2)}) copy-start(bf16[4,192,768]{2,1,0:T(8,128)(2,1)S(1)} %get-tuple-element.14.high) | copy-start | bytes 3538948
  4.6 29.5 %copy-start.5 = (bf16[192,128]{1,0:T(8,128)(2,1)}, bf16[192,128]{1,0:T(8,128)(2,1)S(1)}, u32[]{:S(2)}) copy-start(bf16[192,128]{1,0:T(8,128)(2,1)S(1)} %get-tuple-element.17.own) | copy-start | bytes 147460
  4.6 37.9 %collective-permute-start = (bf16[4,192,768]{2,1,0:T(8,128)(2,1)S(1)}, bf16[4,192,768]{2,1,0:T(8,128)(2,1)}, u32[]{:S(2)}, u32[]{:S(2)}) collective-permute-start(bf16[4,192,768]{2,1,0:T(8,128)(2,1)S(1)} %get-tuple-element.14.high), channel_id=1, source_target_pairs={{0,1},{1,2},{2,3},{3,4},{4,5},{5,6},{6,7},{7,8},{8,9},{9,10},{10,1... | collective-permute-start | bytes 3538952 | tf_op jit(solution)/shard_map/ppermute | solution.py:494
  7.2 35.2 %collective-permute-start.1 = (bf16[4,192,768]{2,1,0:T(8,128)(2,1)S(1)}, bf16[4,192,768]{2,1,0:T(8,128)(2,1)}, u32[]{:S(2)}, u32[]{:S(2)}) collective-permute-start(bf16[4,192,768]{2,1,0:T(8,128)(2,1)S(1)} %get-tuple-element.13.low), channel_id=1, source_target_pairs={{0,127},{1,0},{2,1},{3,2},{4,3},{5,4},{6,5},{7,6},{8,7},{9,8},{10,... | collective-permute-start | bytes 3538952 | tf_op jit(solution)/shard_map/ppermute | solution.py:495
  24.7 30.3 %collective-permute-start.4 = (bf16[192,128]{1,0:T(8,128)(2,1)S(1)}, bf16[192,128]{1,0:T(8,128)(2,1)S(1)}, u32[]{:S(2)}, u32[]{:S(2)}) collective-permute-start(bf16[192,128]{1,0:T(8,128)(2,1)S(1)} %get-tuple-element.17.own), channel_id=1, source_target_pairs={{0,3},{2,5},{4,7},{6,9},{8,11},{10,13},{12,15},{14,17},{16,19},{18... | collective-permute-start | bytes 147464 | tf_op jit(solution)/shard_map/ppermute | solution.py:502
  33.6 21.4 %collective-permute-start.3 = (bf16[192,128]{1,0:T(8,128)(2,1)S(1)}, bf16[192,128]{1,0:T(8,128)(2,1)S(1)}, u32[]{:S(2)}, u32[]{:S(2)}) collective-permute-start(bf16[192,128]{1,0:T(8,128)(2,1)S(1)} %get-tuple-element.17.own), channel_id=1, source_target_pairs={{0,126},{1,127},{2,0},{3,1},{4,2},{5,3},{6,4},{7,5},{8,6},{9,7},{1... | collective-permute-start | bytes 147464 | tf_op jit(solution)/shard_map/ppermute | solution.py:500
  34.1 20.9 %collective-permute-start.2 = (bf16[192,128]{1,0:T(8,128)(2,1)S(1)}, bf16[192,128]{1,0:T(8,128)(2,1)S(1)}, u32[]{:S(2)}, u32[]{:S(2)}) collective-permute-start(bf16[192,128]{1,0:T(8,128)(2,1)S(1)} %get-tuple-element.17.own), channel_id=1, source_target_pairs={{0,2},{1,3},{2,4},{3,5},{4,6},{5,7},{6,8},{7,9},{8,10},{9,11},{10,... | collective-permute-start | bytes 147464 | tf_op jit(solution)/shard_map/ppermute | solution.py:499
  35.1 19.9 %all-to-all-start = ((f32[128,1,128]{2,1,0:T(1,128)}), f32[128,1,128]{2,1,0:T(1,128)S(1)}, u32[]{:S(2)}, u32[]{:S(2)}) async-start(f32[128,1,128]{2,1,0:T(1,128)} %bitcast.3), calls=%async_computation | async-start | bytes 131072 | tf_op jit(solution)/shard_map/all_to_all | solution.py:496
  55.0 0.6 copy-start.7
  55.0 0.6 copy-start.8
  55.0 0.6 copy-start.9
  55.0 0.6 copy-start.6

commit v5 on v4

--- a/solution.py
+++ b/solution.py
@@ -262,16 +262,22 @@
 
 def near_outer_kernel(count, place, low, high, below, above, outer_in, near_in, near, parts, held, made, outer, sems):
     kept = flags(place[0], count)
-    weights = pltpu.make_async_copy(outer_in, outer, sems.at[0])
-    inner_part = pltpu.make_async_copy(near_in, near, sems.at[1])
-    weights.start()
+    weights = [
+        pltpu.make_async_copy(outer_in.at[4 * m : 4 * m + 4], outer.at[4 * m : 4 * m + 4], sems.at[m])
+        for m in range(4)
+    ]
+    inner_part = pltpu.make_async_copy(near_in, near, sems.at[4])
+    for b in range(4):
+        weights[MIRROR[b]].start()
     inner_part.start()
     spread(below, high, lambda d0, d2: d0 * kept[0] - d2, parts, 0)
     spread(low, above, lambda d1, d3: d1 - d3 * kept[1], parts, 16)
-    weights.wait()
-    gathered_products(
-        lambda b, c: mul_t(parts[b * 4 + c], outer[MIRROR[b] * 4 + MIRROR[c]]), held, made
-    )
+    def mirrored(b, c):
+        if c == 0:
+            weights[MIRROR[b]].wait()
+        return mul_t(parts[b * 4 + c], outer[MIRROR[b] * 4 + MIRROR[c]])
+
+    gathered_products(mirrored, held, made)
     inner_part.wait()
     near[0] += held[...]
     gathered_products(lambda b, c: mul(parts[16 + b * 4 + c], outer[b * 4 + c]), held, made)
@@ -290,7 +296,7 @@
             pltpu.VMEM((2, 2, ROWS, PTS), F32),
             pltpu.VMEM((16, ROWS, PTS), F32),
             pltpu.VMEM((16, PTS, PTS), BF16),
-            pltpu.SemaphoreType.DMA((2,)),
+            pltpu.SemaphoreType.DMA((5,)),
         ],
         cost_estimate=pl.CostEstimate(flops=7_000_000_000, bytes_accessed=20_000_000, transcendentals=0),
         compiler_params=pltpu.CompilerParams(vmem_limit_bytes=60 << 20),

time: 76 us -> 76 us (level)
  no operation moved by 1% of the time
where the time goes in v5:
time: 76 us; the launch traced here: 75.8 us
  Pallas kernels  51.7 us (68%)
  starting transfers between devices  20.4 us (27%)
  local copies, waits for them, and re-layouts  2.64 us (3%)
    pallas_call x1, Pallas kernels, transfer(): pl.pallas_call(functools.partial(transfer_kernel, count), name='transfer'...  19.9 us
    pallas_call x1, Pallas kernels, near_inner(): pl.pallas_call(near_inner_kernel, name='near_inner', out_shape=(jax.Shape...  17.4 us
    pallas_call x1, Pallas kernels, near_outer(): pl.pallas_call(functools.partial(near_outer_kernel, count), name='near_ou...  12.5 us
    ppermute x1, starting transfers between devices, body(): far3 = lax.ppermute(own, 'leaf', crossed + [(j, i) for i, j in crossed])  8.9 us
    all_to_all x1, starting transfers between devices, body(): charge = lax.all_to_all(partial, 'leaf', 0, 0, tiled=True)  7.33 us
    ppermute x1, starting transfers between devices, body(): below = lax.ppermute(high, 'leaf', around(count, 1))  2.69 us
    unnamed x22, local copies, waits for them, and re-layouts  2.47 us
    pallas_call x1, Pallas kernels, prologue(): pl.pallas_call(prologue_kernel, name='prologue', out_shape=(pack, pack, j...  1.76 us
  transfers between devices with their start and end apart: 6, of which 0 were waited for; matrix products, arithmetic and copies ran while one was open for 0% of the time, Pallas kernels for 40%

profile of v5, /device:TPU:1, one launch (start us, length us, event | category | flops | bytes accessed | tf_op | source)
XLA Modules:
  0.0 75.8 jit_solution(14750305608999058046)
XLA Ops:
  0.0 0.7 convert_element_type.8
  0.8 0.1 broadcast_in_dim.7
  0.8 1.8 %copy.8.density = bf16[2,24,28,512]{3,2,1,0:T(8,128)(2,1)S(1)} copy(bf16[2,24,28,512]{3,1,2,0:T(8,128)(2,1)} %param.6) | data formatting | bytes 2752512 | tf_op args[0]
  2.7 0.1 broadcast_in_dim.8.mask
  2.8 1.8 %prologue.1 = (bf16[4,192,768]{2,1,0:T(8,128)(2,1)S(1)}, bf16[4,192,768]{2,1,0:T(8,128)(2,1)S(1)}, bf16[192,128]{1,0:T(8,128)(2,1)S(1)}, f32[128,128]{1,0:T(8,128)}) custom-call(bf16[2,24,28,512]{3,2,1,0:T(8,128)(2,1)S(1)} %copy.8.density, f32[192,128]{1,0:T(8,128)S(1)} %broadcast_in_dim.8.mask, bf16[512,128]{1,0:T(8,128)(2,1)S(1)} %copy-done.2, ...), custom_call_target="tpu_custom_call" | custom-call | tf_op jit(solution)/shard_map/prologue/pallas_call | solution.py:74
  4.6 2.7 %collective-permute-start = (bf16[4,192,768]{2,1,0:T(8,128)(2,1)S(1)}, bf16[4,192,768]{2,1,0:T(8,128)(2,1)}, u32[]{:S(2)}, u32[]{:S(2)}) collective-permute-start(bf16[4,192,768]{2,1,0:T(8,128)(2,1)S(1)} %get-tuple-element.14.high), channel_id=1, source_target_pairs={{0,1},{1,2},{2,3},{3,4},{4,5},{5,6},{6,7},{7,8},{8,9},{9,10},{10,1... | collective-permute-start | bytes 3538952 | tf_op jit(solution)/shard_map/ppermute | solution.py:500
  7.2 0.0 collective-permute-start.1
  7.3 17.4 %near_inner.1 = (f32[2,2,2,192,512]{4,3,2,1,0:T(8,128)}, bf16[16,512,512]{2,1,0:T(8,128)(2,1)}) custom-call(bf16[4,192,768]{2,1,0:T(8,128)(2,1)} %copy-done.3, bf16[4,192,768]{2,1,0:T(8,128)(2,1)} %copy-done.4, bf16[14,512,512]{2,1,0:T(8,128)(2,1)} %tables_in.2), custom_call_target="tpu_custom_call" | custom-call | flops 10000000000 | bytes 20000000 | tf_op jit(solution)/shard_map/near_inner/pallas_call | solution.py:234
  24.7 8.9 %collective-permute-start.4 = (bf16[192,128]{1,0:T(8,128)(2,1)S(1)}, bf16[192,128]{1,0:T(8,128)(2,1)S(1)}, u32[]{:S(2)}, u32[]{:S(2)}) collective-permute-start(bf16[192,128]{1,0:T(8,128)(2,1)S(1)} %get-tuple-element.17.own), channel_id=1, source_target_pairs={{0,3},{2,5},{4,7},{6,9},{8,11},{10,13},{12,15},{14,17},{16,19},{18... | collective-permute-start | bytes 147464 | tf_op jit(solution)/shard_map/ppermute | solution.py:508
  33.6 0.5 collective-permute-start.3
  34.1 1.0 %collective-permute-start.2 = (bf16[192,128]{1,0:T(8,128)(2,1)S(1)}, bf16[192,128]{1,0:T(8,128)(2,1)S(1)}, u32[]{:S(2)}, u32[]{:S(2)}) collective-permute-start(bf16[192,128]{1,0:T(8,128)(2,1)S(1)} %get-tuple-element.17.own), channel_id=1, source_target_pairs={{0,2},{1,3},{2,4},{3,5},{4,6},{5,7},{6,8},{7,9},{8,10},{9,11},{10,... | collective-permute-start | bytes 147464 | tf_op jit(solution)/shard_map/ppermute | solution.py:505
  35.1 7.3 %all-to-all-start = ((f32[128,1,128]{2,1,0:T(1,128)}), f32[128,1,128]{2,1,0:T(1,128)S(1)}, u32[]{:S(2)}, u32[]{:S(2)}) async-start(f32[128,1,128]{2,1,0:T(1,128)} %bitcast.3), calls=%async_computation | async-start | bytes 131072 | tf_op jit(solution)/shard_map/all_to_all | solution.py:502
  42.4 0.0 collective-permute-done.below
  42.4 0.0 collective-permute-done.1.above
  42.5 12.5 %near_outer.1.near_in = f32[2,2,2,192,512]{4,3,2,1,0:T(8,128)} custom-call(s32[1]{0:T(128)} %bitcast.place, bf16[4,192,768]{2,1,0:T(8,128)(2,1)} %copy-done.3, bf16[4,192,768]{2,1,0:T(8,128)(2,1)} %copy-done.4, bf16[4,192,768]{2,1,0:T(8,128)(2,1)} %collective-permute-done.below, bf16[4,192,768]{2,1,0:T(8,128)(2,1)} %collective-permute-done.1.above, ...), custom_call_target="tpu_custom_call" | custom-call | flops 7000000000 | bytes 20000000 | tf_op jit(solution)/shard_map/near_outer/pallas_call | solution.py:288
  55.0 0.0 collective-permute-done.4.far3
  55.0 0.0 collective-permute-done.3.ahead2
  55.1 0.0 collective-permute-done.2.back2
  55.1 0.0 all-to-all-done
  55.1 0.5 copy-done.7
  55.6 0.0 copy-done.8
  55.7 0.0 copy-done.9
  55.7 0.0 copy-done.6
  55.7 19.9 %transfer.1 = bf16[2,28,24,512]{3,2,1,0:T(8,128)(2,1)} custom-call(s32[1]{0:T(128)} %bitcast.place, bf16[4,192,768]{2,1,0:T(8,128)(2,1)} %copy-done.3, bf16[4,192,768]{2,1,0:T(8,128)(2,1)} %collective-permute-done.below, bf16[4,192,768]{2,1,0:T(8,128)(2,1)} %collective-permute-done.1.above, bf16[192,128]{1,0:T(8,128)(2,1)} %copy-done.5, ...), custom_call_target="tpu_custom_call" | custom-call | flops 12000000000 | bytes 20000000 | tf_op jit(solution)/shard_map/transfer/pallas_call | solution.py:466
  (18 shorter events, 0.0 us)
Async XLA Ops:
  0.0 2.8 %copy-start.2 = (bf16[512,128]{1,0:T(8,128)(2,1)S(1)}, bf16[512,128]{1,0:T(8,128)(2,1)}, u32[]{:S(2)}) copy-start(bf16[512,128]{1,0:T(8,128)(2,1)} %anterpolate.3) | copy-start | bytes 393220
  0.0 2.8 %copy-start.1 = (bf16[8,128,128]{2,1,0:T(8,128)(2,1)S(1)}, bf16[8,128,128]{2,1,0:T(8,128)(2,1)}, u32[]{:S(2)}) copy-start(bf16[8,128,128]{2,1,0:T(8,128)(2,1)} %param.9) | copy-start | bytes 786436
  2.8 21.9 %copy-start = (f32[192,128]{1,0:T(8,128)}, f32[192,128]{1,0:T(8,128)S(1)}, u32[]{:S(2)}) copy-start(f32[192,128]{1,0:T(8,128)S(1)} %broadcast_in_dim.8.mask) | copy-start | bytes 294916
  4.6 2.7 %copy-start.3 = (bf16[4,192,768]{2,1,0:T(8,128)(2,1)}, bf16[4,192,768]{2,1,0:T(8,128)(2,1)S(1)}, u32[]{:S(2)}) copy-start(bf16[4,192,768]{2,1,0:T(8,128)(2,1)S(1)} %get-tuple-element.13.low) | copy-start | bytes 3538948
  4.6 2.7 %copy-start.4 = (bf16[4,192,768]{2,1,0:T(8,128)(2,1)}, bf16[4,192,768]{2,1,0:T(8,128)(2,1)S(1)}, u32[]{:S(2)}) copy-start(bf16[4,192,768]{2,1,0:T(8,128)(2,1)S(1)} %get-tuple-element.14.high) | copy-start | bytes 3538948
  4.6 29.5 %copy-start.5 = (bf16[192,128]{1,0:T(8,128)(2,1)}, bf16[192,128]{1,0:T(8,128)(2,1)S(1)}, u32[]{:S(2)}) copy-start(bf16[192,128]{1,0:T(8,128)(2,1)S(1)} %get-tuple-element.17.own) | copy-start | bytes 147460
  4.6 37.9 %collective-permute-start = (bf16[4,192,768]{2,1,0:T(8,128)(2,1)S(1)}, bf16[4,192,768]{2,1,0:T(8,128)(2,1)}, u32[]{:S(2)}, u32[]{:S(2)}) collective-permute-start(bf16[4,192,768]{2,1,0:T(8,128)(2,1)S(1)} %get-tuple-element.14.high), channel_id=1, source_target_pairs={{0,1},{1,2},{2,3},{3,4},{4,5},{5,6},{6,7},{7,8},{8,9},{9,10},{10,1... | collective-permute-start | bytes 3538952 | tf_op jit(solution)/shard_map/ppermute | solution.py:500
  7.2 35.2 %collective-permute-start.1 = (bf16[4,192,768]{2,1,0:T(8,128)(2,1)S(1)}, bf16[4,192,768]{2,1,0:T(8,128)(2,1)}, u32[]{:S(2)}, u32[]{:S(2)}) collective-permute-start(bf16[4,192,768]{2,1,0:T(8,128)(2,1)S(1)} %get-tuple-element.13.low), channel_id=1, source_target_pairs={{0,127},{1,0},{2,1},{3,2},{4,3},{5,4},{6,5},{7,6},{8,7},{9,8},{10,... | collective-permute-start | bytes 3538952 | tf_op jit(solution)/shard_map/ppermute | solution.py:501
  24.7 30.3 %collective-permute-start.4 = (bf16[192,128]{1,0:T(8,128)(2,1)S(1)}, bf16[192,128]{1,0:T(8,128)(2,1)S(1)}, u32[]{:S(2)}, u32[]{:S(2)}) collective-permute-start(bf16[192,128]{1,0:T(8,128)(2,1)S(1)} %get-tuple-element.17.own), channel_id=1, source_target_pairs={{0,3},{2,5},{4,7},{6,9},{8,11},{10,13},{12,15},{14,17},{16,19},{18... | collective-permute-start | bytes 147464 | tf_op jit(solution)/shard_map/ppermute | solution.py:508
  33.6 21.4 %collective-permute-start.3 = (bf16[192,128]{1,0:T(8,128)(2,1)S(1)}, bf16[192,128]{1,0:T(8,128)(2,1)S(1)}, u32[]{:S(2)}, u32[]{:S(2)}) collective-permute-start(bf16[192,128]{1,0:T(8,128)(2,1)S(1)} %get-tuple-element.17.own), channel_id=1, source_target_pairs={{0,126},{1,127},{2,0},{3,1},{4,2},{5,3},{6,4},{7,5},{8,6},{9,7},{1... | collective-permute-start | bytes 147464 | tf_op jit(solution)/shard_map/ppermute | solution.py:506
  34.1 21.0 %collective-permute-start.2 = (bf16[192,128]{1,0:T(8,128)(2,1)S(1)}, bf16[192,128]{1,0:T(8,128)(2,1)S(1)}, u32[]{:S(2)}, u32[]{:S(2)}) collective-permute-start(bf16[192,128]{1,0:T(8,128)(2,1)S(1)} %get-tuple-element.17.own), channel_id=1, source_target_pairs={{0,2},{1,3},{2,4},{3,5},{4,6},{5,7},{6,8},{7,9},{8,10},{9,11},{10,... | collective-permute-start | bytes 147464 | tf_op jit(solution)/shard_map/ppermute | solution.py:505
  35.1 20.0 %all-to-all-start = ((f32[128,1,128]{2,1,0:T(1,128)}), f32[128,1,128]{2,1,0:T(1,128)S(1)}, u32[]{:S(2)}, u32[]{:S(2)}) async-start(f32[128,1,128]{2,1,0:T(1,128)} %bitcast.3), calls=%async_computation | async-start | bytes 131072 | tf_op jit(solution)/shard_map/all_to_all | solution.py:502
  55.0 0.6 copy-start.7
  55.0 0.6 copy-start.8
  55.1 0.6 copy-start.9
  55.1 0.6 copy-start.6
